TPU v7x, 32 devices: a whole 2x2x4 slice. The times are simulated.
32 devices in a mesh: facet: 8 (over z, x), uv: 4 (over y, core).
Axes of the slice: x: 2, y: 2, z: 4, core: 2. Of those that a mesh axis runs over, the one named last changes fastest.
Arguments:
- sky_image: bfloat16 [128, 16384], P('uv', 'facet'), may hold values from -6 to 6
- subgrid_offsets: int32 [8], replicated, may hold values from 0 to 2047
- owner_order: int32 [8], replicated, may hold values from 0 to 7, each once
- visibility_count: int32 [8], P('facet'), may hold values from 1 to 512, 2048 in all
- visibility_cell: int32 [8, 512], P('facet'), may hold values from 0 to 255
- observed: bfloat16 [8, 2, 128, 512], P('facet', None, 'uv'), may hold values from -6 to 6
- visibility_weight: float32 [8, 128, 512], P('facet', 'uv'), may hold values from 0.3 to 3
- row_kernel: float32 [7], replicated, may hold values from 0.3 to 1
- column_kernel: float32 [7], replicated, may hold values from 0.3 to 1
Outputs:
- weighted_residual: float32 [8, 2, 128, 512], P('facet', None, 'uv')
- dirty_image: float32 [128, 16384], P('uv', 'facet')
Inputs may be any that keep to these rules, and one draw needn't show every extreme that they name: `owner_order`: a permutation of the 8 subgrids over the slots. `visibility_count`: the counts sum to 2048, and some slot has exactly 512 live visibilities in every draw.
All inputs are finite; a program needn't handle non-finite values. No bound on the sum of `visibility_count` on one device may be relied on, other than what follows from the above.
Results may differ from a plain program's by a relative error of at most 0.022.
Values may be sent and summed in bfloat16 or wider, within the bound.
A program may use at most 64 MiB of HBM per device.

v0:
```python
import math

import jax
import jax.numpy as jnp
from jax import lax
from jax.sharding import PartitionSpec as P

XC = 128
SG = 256


def padded_2(value, sides, width):
    for axis, dim in sides:
        count, length = (lax.axis_size(axis), value.shape[dim])
        up = [(i, (i + 1) % count) for i in range(count - 1)]
        down = [(j, i) for i, j in up]
        last = lax.slice_in_dim(value, length - width, length, axis=dim)
        first = lax.slice_in_dim(value, 0, width, axis=dim)
        before = lax.ppermute(last, axis, up)
        after = lax.ppermute(first, axis, down)
        value = jnp.concatenate([before, value, after], axis=dim)
    return value


def taper_values(strip_rows):
    position = jnp.arange(strip_rows, dtype=jnp.float32)
    return jnp.sin((position + 0.5) * (math.pi / strip_rows)) / math.sqrt(strip_rows)


def shift_values(slot_offsets, strip_rows):
    position = jnp.arange(strip_rows, dtype=jnp.int32)
    shifted = jnp.bitwise_and(slot_offsets[:, None] * position[None, :], strip_rows - 1)
    angle_shift = shifted.astype(jnp.float32) * (2.0 * math.pi / strip_rows)
    return jnp.stack([jnp.cos(angle_shift), -jnp.sin(angle_shift)], axis=1)


def base_tables(coarse, strip_rows):
    position = jnp.arange(strip_rows, dtype=jnp.int32)
    base = jnp.bitwise_and(
        jnp.arange(coarse, dtype=jnp.int32)[:, None] * position[None, :], strip_rows - 1
    )
    angle_base = base.astype(jnp.float32) * (2.0 * math.pi / strip_rows)
    cosine = jnp.cos(angle_base)
    sine_part = jnp.sin(angle_base)
    upper = jnp.stack([cosine, sine_part])
    lower = jnp.stack([-sine_part, cosine])
    return jnp.stack([upper, lower]).astype(jnp.bfloat16)


def expand_tables(facet, coarse, strip_rows, facet_count):
    grid_width = 2 * coarse
    image_rows = strip_rows * facet_count
    fine_index = jnp.arange(grid_width, dtype=jnp.int32)[:, None]
    coarse_index = jnp.arange(coarse, dtype=jnp.int32)[None, :]
    centre = (facet * strip_rows + strip_rows // 2)[..., None, None]
    product = jnp.bitwise_and(
        jnp.bitwise_and(fine_index * coarse_index, grid_width - 1) * (image_rows // grid_width)
        + (fine_index - 2 * coarse_index) * centre,
        image_rows - 1,
    )
    radians = product.astype(jnp.float32) * (2.0 * math.pi / image_rows)
    factor = 1.0 / math.sqrt(facet_count * coarse)
    cosine = jnp.cos(radians) * factor
    sine_part = jnp.sin(radians) * factor
    upper = jnp.stack([cosine, -sine_part], axis=-3)
    lower = jnp.stack([sine_part, cosine], axis=-3)
    return jnp.stack([upper, lower], axis=-4).astype(jnp.bfloat16)


def degrid_matrix(positions, kernel, grid_width):
    margin = (kernel.shape[0] - 1) // 2
    distance = jnp.arange(grid_width, dtype=jnp.int32)[None, :] - positions[:, None] + margin
    matrix = jnp.zeros(distance.shape, jnp.float32)
    for tap_index in range(kernel.shape[0]):
        matrix = matrix + jnp.where(distance == tap_index, kernel[tap_index], 0.0)
    return matrix.astype(jnp.bfloat16)


def convolve(padded, kernel, columns, flipped):
    tap_count = kernel.shape[0]
    result = jnp.zeros(padded.shape[:-2] + (columns, padded.shape[-1]), jnp.float32)
    for tap_index in range(tap_count):
        first_column = tap_count - 1 - tap_index if flipped else tap_index
        result = result + kernel[tap_index] * padded[..., first_column : first_column + columns, :]
    return result


def visibility_rows(degrid_table, grid_values, observed_slot, weights, live_count):
    model_rows = jnp.einsum(
        "vj,pcj->pcv", degrid_table, grid_values, preferred_element_type=jnp.float32
    )
    row_index = jnp.arange(degrid_table.shape[0], dtype=jnp.int32)
    live_rows = (row_index < live_count).astype(jnp.float32)
    residual = (
        live_rows[None, None, :]
        * weights[None, :, :]
        * (observed_slot.astype(jnp.float32) - model_rows)
    )
    gridded = jnp.einsum(
        "vj,pcv->pcj",
        degrid_table,
        residual.astype(jnp.bfloat16),
        preferred_element_type=jnp.float32,
    )
    return (residual, gridded)


def local(
    sky_image,
    subgrid_offsets,
    owner_order,
    visibility_count,
    visibility_cell,
    observed,
    visibility_weight,
    row_kernel,
    column_kernel,
):
    facet_count = lax.axis_size("facet")
    facet_index = lax.axis_index("facet")
    columns, strip_rows = sky_image.shape
    owned_slots = visibility_count.shape[0]
    margin = (column_kernel.shape[0] - 1) // 2
    window_taper = taper_values(strip_rows)
    windowed = (sky_image.astype(jnp.float32) * window_taper[None, :]).astype(jnp.bfloat16)
    slot_offset = subgrid_offsets[owner_order]
    shift_table = shift_values(slot_offset, strip_rows)
    base_table = base_tables(XC, strip_rows)
    own_table = expand_tables(facet_index, XC, strip_rows, facet_count)
    modulated = (
        shift_table[:, :, None, :] * windowed.astype(jnp.float32)[None, None, :, :]
    ).astype(jnp.bfloat16)
    contribution = jnp.einsum(
        "pqkr,iqcr->ipck", base_table, modulated, preferred_element_type=jnp.float32
    ).astype(jnp.bfloat16)
    all_tables = expand_tables(
        jnp.arange(facet_count, dtype=jnp.int32), XC, strip_rows, facet_count
    )
    arrived = lax.all_to_all(contribution, "facet", split_axis=0, concat_axis=0, tiled=True)
    arrived = arrived.reshape(facet_count, owned_slots, 2, columns, XC)
    subgrid = jnp.einsum(
        "fpqjk,fsqck->spcj", all_tables, arrived, preferred_element_type=jnp.float32
    )
    padded = padded_2(subgrid.astype(jnp.bfloat16), (("uv", 2),), margin).astype(subgrid.dtype)
    grid_values = convolve(padded, column_kernel, columns, False).astype(jnp.bfloat16)
    degrid_table = degrid_matrix(visibility_cell[0], row_kernel, SG)
    live_count = visibility_count[0]
    observed_slot = observed[0]
    weights = visibility_weight[0]
    target = grid_values[0]
    residual, gridded = visibility_rows(degrid_table, target, observed_slot, weights, live_count)
    residual_parts = [residual]
    gridded_parts = [gridded]
    residuals = jnp.stack(residual_parts)
    gridded = jnp.stack(gridded_parts)
    padded_back = padded_2(gridded.astype(jnp.bfloat16), (("uv", 2),), margin).astype(gridded.dtype)
    back_grid = convolve(padded_back, column_kernel, columns, True).astype(jnp.bfloat16)
    back_pieces = jnp.einsum(
        "qpjk,sqcj->spck",
        own_table,
        lax.all_gather(back_grid, "facet", axis=0, tiled=True),
        preferred_element_type=jnp.float32,
    ).astype(jnp.bfloat16)
    back_rows = jnp.einsum(
        "pqkr,ipck->iqcr", base_table, back_pieces, preferred_element_type=jnp.float32
    )
    dirty_sum = jnp.einsum("iqr,iqcr->cr", shift_table, back_rows)
    return (residuals, dirty_sum * window_taper[None, :])


def solution(mesh):
    in_specs = (
        P("uv", "facet"),
        P(),
        P(),
        P("facet"),
        P("facet", None),
        P("facet", None, "uv", None),
        P("facet", "uv", None),
        P(),
        P(),
    )
    out_specs = (P("facet", None, "uv", None), P("uv", "facet"))
    return jax.shard_map(local, mesh=mesh, in_specs=in_specs, out_specs=out_specs, check_vma=False)
```

profile of v0, /device:TPU:0, one launch (start us, length us, event | category | flops | bytes accessed | tf_op | source)
XLA Modules:
  0.0 93.4 jit_solution(3858125224354690558)
XLA Ops:
  0.6 0.0 copy-start
  0.7 3.9 %negate_convert_fusion.1 = (bf16[1,128,2048]{2,1,0:T(8,128)(2,1)S(1)}, bf16[1,128,2048]{2,1,0:T(8,128)(2,1)S(1)}) fusion(), kind=kLoop, calls=%fused_computation.38 | loop fusion | flops 1835008 | bytes 1048576 | tf_op jit(solution)/shard_map/convert.20
  4.6 0.0 copy-start.3
  4.6 3.6 %fusion.43 = bf16[1,128,2048]{2,1,0:T(8,128)(2,1)S(1)} fusion(), kind=kLoop, calls=%fused_computation.42 | loop fusion | flops 1310720 | bytes 524288 | tf_op jit(solution)/shard_map/convert.24
  8.1 0.1 sine_multiply_fusion.2
  8.2 0.6 gather_fusion
  8.9 0.3 fusion.84
  9.2 0.1 copy.14
  9.4 0.2 maximum_bitcast_fusion
  9.6 1.0 %copy-done.1 = bf16[1,2,128,2048]{3,2,1,0:T(8,128)(2,1)} copy-done((bf16[1,2,128,2048]{3,2,1,0:T(8,128)(2,1)}, bf16[1,2,128,2048]{3,2,1,0:T(8,128)(2,1)S(1)}, u32[]{:S(2)}) %copy-start.1) | copy-done | bytes 1048600
  10.6 1.4 %fusion.24 = bf16[8,2,32,128]{3,2,1,0:T(8,128)(2,1)} fusion(f32[32,2048]{1,0:T(8,128)S(1)} %fusion.66, f32[8,2,2048]{2,1,0:T(2,128)S(1)} %copy.14, bf16[1,2,128,2048]{3,2,1,0:T(8,128)(2,1)S(1)} %get-tuple-element.3, bf16[1,2,128,2048]{3,2,1,0:T(8,128)(2,1)S(1)} %get-tuple-element.2), kind=kOutput, calls=%fused_computation.20 | convolution fusion | flops 543227904 | bytes 2621440 | tf_op jit(solution)/shard_map/pqkr,iqcr->ipck/dot_general | solution.py:133
  12.0 7.3 %all-to-all-start = ((bf16[8,2,32,128]{3,2,1,0:T(8,128)(2,1)}), bf16[8,2,32,128]{3,2,1,0:T(8,128)(2,1)}, u32[]{:S(2)}, u32[]{:S(2)}) async-start(bf16[8,2,32,128]{3,2,1,0:T(8,128)(2,1)} %fusion.24), calls=%async_computation | async-start | bytes 262144 | tf_op jit(solution)/shard_map/all_to_all | solution.py:139
  19.3 0.7 fusion.116
  20.7 4.2 %negate_convert_fusion = (bf16[8,1,256,128]{3,2,1,0:T(8,128)(2,1)S(1)}, bf16[8,1,256,128]{3,2,1,0:T(8,128)(2,1)S(1)}, bf16[8,1,256,128]{3,2,1,0:T(8,128)(2,1)S(1)}) fusion(s32[8]{0:T(128)S(1)} %multiply_add_fusion, s32[256,128]{1,0:T(8,128)S(1)} %get-tuple-element.36, s32[256,128]{1,0:T(8,128)S(1)} %get-tuple-element.37), kind=kLoop, calls=%fused_computation.33 | loop fusion | flops 2883584 | bytes 1835040 | tf_op jit(solution)/shard_map/convert.16
  24.9 0.2 maximum_bitcast_fusion.2
  25.0 0.5 negate_convert_fusion.2
  25.6 1.2 %all-to-all-done = bf16[8,2,32,128]{3,2,1,0:T(8,128)(2,1)} async-done(((bf16[8,2,32,128]{3,2,1,0:T(8,128)(2,1)}), bf16[8,2,32,128]{3,2,1,0:T(8,128)(2,1)}, u32[]{:S(2)}, u32[]{:S(2)}) %all-to-all-start) | async-done | bytes 131104 | tf_op jit(solution)/shard_map/all_to_all | solution.py:139
  26.7 1.6 %fusion.38 = bf16[1,2,32,256]{3,2,1,0:T(8,128)(2,1)S(1)} fusion(bf16[8,1,2,256,128]{4,3,2,1,0:T(8,128)(2,1)S(1)} %get-tuple-element.5, bf16[8,1,2,256,128]{4,3,2,1,0:T(8,128)(2,1)S(1)} %get-tuple-element.4, bf16[8,2,32,128]{3,2,1,0:T(8,128)(2,1)} %all-to-all-done), kind=kOutput, calls=%fused_computation.28 | convolution fusion | flops 71319552 | bytes 2260992 | tf_op jit(solution)/shard_map/fpqjk,fsqck->spcj/dot_general | solution.py:141
  28.4 1.3 %collective-permute-start = (bf16[1,2,3,256]{3,2,1,0:T(4,128)(2,1)S(1)}, bf16[1,2,3,256]{3,2,1,0:T(4,128)(2,1)S(1)}, u32[]{:S(2)}, u32[]{:S(2)}) collective-permute-start(bf16[1,2,3,256]{3,2,1,0:T(4,128)(2,1)S(1)} %get-tuple-element.15), channel_id=1, source_target_pairs={{0,1},{1,2},{2,3},{4,5},{5,6},{6,7},{8,9},{9,10},{10,11},{12,13},{... | collective-permute-start | bytes 9224 | tf_op jit(solution)/shard_map/ppermute | solution.py:19
  29.7 1.3 %collective-permute-start.1 = (bf16[1,2,3,256]{3,2,1,0:T(4,128)(2,1)S(1)}, bf16[1,2,3,256]{3,2,1,0:T(4,128)(2,1)S(1)}, u32[]{:S(2)}, u32[]{:S(2)}) collective-permute-start(bf16[1,2,3,256]{3,2,1,0:T(4,128)(2,1)S(1)} %get-tuple-element.16), channel_id=1, source_target_pairs={{1,0},{2,1},{3,2},{5,4},{6,5},{7,6},{9,8},{10,9},{11,10},{13,12},{... | collective-permute-start | bytes 9224 | tf_op jit(solution)/shard_map/ppermute | solution.py:20
  31.0 0.7 fusion.117
  31.7 2.8 %collective-permute-done.1 = bf16[1,2,3,256]{3,2,1,0:T(4,128)(2,1)S(1)} collective-permute-done((bf16[1,2,3,256]{3,2,1,0:T(4,128)(2,1)S(1)}, bf16[1,2,3,256]{3,2,1,0:T(4,128)(2,1)S(1)}, u32[]{:S(2)}, u32[]{:S(2)}) %collective-permute-start.1) | collective-permute-done | bytes 3104 | tf_op jit(solution)/shard_map/ppermute | solution.py:20
  34.5 9.3 %fusion.30 = f32[2,32,512]{2,1,0:T(8,128)S(1)} fusion(f32[]{:T(128)} %bitcast.38, f32[]{:T(128)} %bitcast.37, f32[]{:T(128)} %bitcast.36, f32[]{:T(128)} %bitcast.35, f32[]{:T(128)} %bitcast.34, f32[]{:T(128)} %bitcast.33, f32[]{:T(128)} %bitcast.32, s32[512]{0:T(512)S(1)} %bitcast.137, bf16[1,2,32,512]{3,2,1,0:T(8,128)(2,1)S(1)} %copy-done.7, ...), kind=kOutput, calls=%fused_computation.23 | convolution fusion | flops 20119552 | bytes 723000 | tf_op jit(solution)/shard_map/vj,pcj->pcv/dot_general | solution.py:89
  43.9 4.8 %fusion.37 = bf16[1,2,32,256]{3,2,1,0:T(8,128)(2,1)S(1)} fusion(f32[]{:T(128)} %bitcast.38, f32[]{:T(128)} %bitcast.37, f32[]{:T(128)} %bitcast.36, f32[]{:T(128)} %bitcast.35, f32[]{:T(128)} %bitcast.34, f32[]{:T(128)} %bitcast.33, f32[]{:T(128)} %bitcast.32, s32[512]{0:T(512)S(1)} %bitcast.138, f32[2,32,512]{2,1,0:T(8,128)S(1)} %fusion.30), kind=kOutput, calls=%fused_computation.27 | convolution fusion | flops 19841024 | bytes 165916 | tf_op jit(solution)/shard_map/vj,pcv->pcj/dot_general | solution.py:99
  48.8 4.4 %collective-permute-start.2 = (bf16[1,2,3,256]{3,2,1,0:T(4,128)(2,1)S(1)}, bf16[1,2,3,256]{3,2,1,0:T(4,128)(2,1)S(1)}, u32[]{:S(2)}, u32[]{:S(2)}) collective-permute-start(bf16[1,2,3,256]{3,2,1,0:T(4,128)(2,1)S(1)} %get-tuple-element.13), channel_id=1, source_target_pairs={{0,1},{1,2},{2,3},{4,5},{5,6},{6,7},{8,9},{9,10},{10,11},{12,13},{... | collective-permute-start | bytes 9224 | tf_op jit(solution)/shard_map/ppermute | solution.py:19
  53.2 1.3 %collective-permute-start.3 = (bf16[1,2,3,256]{3,2,1,0:T(4,128)(2,1)S(1)}, bf16[1,2,3,256]{3,2,1,0:T(4,128)(2,1)S(1)}, u32[]{:S(2)}, u32[]{:S(2)}) collective-permute-start(bf16[1,2,3,256]{3,2,1,0:T(4,128)(2,1)S(1)} %get-tuple-element.14), channel_id=1, source_target_pairs={{1,0},{2,1},{3,2},{5,4},{6,5},{7,6},{9,8},{10,9},{11,10},{13,12},{... | collective-permute-start | bytes 9224 | tf_op jit(solution)/shard_map/ppermute | solution.py:20
  54.5 0.1 copy.32
  54.6 1.6 %collective-permute-done.3 = bf16[1,2,3,256]{3,2,1,0:T(4,128)(2,1)S(1)} collective-permute-done((bf16[1,2,3,256]{3,2,1,0:T(4,128)(2,1)S(1)}, bf16[1,2,3,256]{3,2,1,0:T(4,128)(2,1)S(1)}, u32[]{:S(2)}, u32[]{:S(2)}) %collective-permute-start.3) | collective-permute-done | bytes 3104 | tf_op jit(solution)/shard_map/ppermute | solution.py:20
  56.3 4.5 %fusion.70 = bf16[1,2,32,256]{3,2,1,0:T(8,128)(2,1)S(1)} fusion(f32[1,2,38,256]{3,2,1,0:T(8,128)S(1)} %maximum_convert_fusion.1, f32[]{:T(128)} %bitcast.29, f32[]{:T(128)} %bitcast.28, f32[]{:T(128)} %bitcast.27, f32[]{:T(128)} %bitcast.26, f32[]{:T(128)} %bitcast.25, f32[]{:T(128)} %bitcast.24, f32[]{:T(128)} %bitcast.5), kind=kLoop, calls=%fused_computation.79 | loop fusion | flops 229376 | bytes 491548 | tf_op jit(solution)/shard_map/convert_element_type | solution.py:157
  60.8 30.8 %all_gather.3 = bf16[8,2,32,256]{3,2,1,0:T(8,128)(2,1)S(1)} all-gather(bf16[1,2,32,256]{3,2,1,0:T(8,128)(2,1)S(1)} %fusion.70), channel_id=1, replica_groups=mesh['facet'=8,'uv'=4] {'facet'}, dimensions={0}, use_global_device_ids=true | all-gather | bytes 294912 | tf_op jit(solution)/shard_map/all_gather | solution.py:161
  91.6 1.0 %fusion = f32[2048,32]{0,1:T(8,128)S(1)} fusion(f32[2048,8,2]{0,2,1:T(2,128)S(1)} %copy.32, bf16[1,2,256,128]{3,2,0,1:T(8,128)(2,1)S(1)} %get-tuple-element.12, bf16[1,2,256,128]{3,2,0,1:T(8,128)(2,1)S(1)} %get-tuple-element.11, bf16[8,2,32,256]{3,2,1,0:T(8,128)(2,1)S(1)} %all_gather.3, bf16[1,2,128,2048]{3,2,1,0:T(8,128)(2,1)S(1)} %copy-done.2, ...), kind=kOutput, calls=%fused_computation.2 | convolution fusion | flops 607649792 | bytes 3014656 | tf_op jit(solution)/shard_map/pqkr,ipck->iqcr/dot_general | solution.py:164
  92.6 0.7 multiply_bitcast_fusion
  (35 shorter events, 0.2 us)
Async XLA Ops:
  0.6 7.6 %copy-start = (s32[8]{0:T(128)S(1)}, s32[8]{0:T(128)}, u32[]{:S(2)}) copy-start(s32[8]{0:T(128)} %param.10) | copy-start | bytes 100
  0.6 7.6 %copy-start.9 = (s32[8]{0:T(128)S(1)}, s32[8]{0:T(128)}, u32[]{:S(2)}) copy-start(s32[8]{0:T(128)} %param.11) | copy-start | bytes 100
  4.6 4.8 %copy-start.3 = (bf16[32,2048]{1,0:T(8,128)(2,1)S(1)}, bf16[32,2048]{1,0:T(8,128)(2,1)}, u32[]{:S(2)}) copy-start(bf16[32,2048]{1,0:T(8,128)(2,1)} %param.9) | copy-start | bytes 393220
  9.6 1.0 %copy-start.1 = (bf16[1,2,128,2048]{3,2,1,0:T(8,128)(2,1)}, bf16[1,2,128,2048]{3,2,1,0:T(8,128)(2,1)S(1)}, u32[]{:S(2)}) copy-start(bf16[1,2,128,2048]{3,2,1,0:T(8,128)(2,1)S(1)} %get-tuple-element.3) | copy-start | bytes 3145732
  10.6 8.7 %copy-start.5 = (f32[7]{0:T(128)S(1)}, f32[7]{0:T(128)}, u32[]{:S(2)}) copy-start(f32[7]{0:T(128)} %param.17) | copy-start | bytes 88
  10.6 10.1 %copy-start.4 = (f32[1,32,512]{2,1,0:T(8,128)S(1)}, f32[1,32,512]{2,1,0:T(8,128)}, u32[]{:S(2)}) copy-start(f32[1,32,512]{2,1,0:T(8,128)} %param.15) | copy-start | bytes 196612
  12.0 14.7 %all-to-all-start = ((bf16[8,2,32,128]{3,2,1,0:T(8,128)(2,1)}), bf16[8,2,32,128]{3,2,1,0:T(8,128)(2,1)}, u32[]{:S(2)}, u32[]{:S(2)}) async-start(bf16[8,2,32,128]{3,2,1,0:T(8,128)(2,1)} %fusion.24), calls=%async_computation | async-start | bytes 262144 | tf_op jit(solution)/shard_map/all_to_all | solution.py:139
  26.7 4.3 %copy-start.6 = (f32[7]{0:T(128)S(1)}, f32[7]{0:T(128)}, u32[]{:S(2)}) copy-start(f32[7]{0:T(128)} %param.16) | copy-start | bytes 88
  26.7 7.8 %copy-start.7 = (bf16[1,2,32,512]{3,2,1,0:T(8,128)(2,1)S(1)}, bf16[1,2,32,512]{3,2,1,0:T(8,128)(2,1)}, u32[]{:S(2)}) copy-start(bf16[1,2,32,512]{3,2,1,0:T(8,128)(2,1)} %param.14) | copy-start | bytes 196612
  26.7 7.8 %copy-start.8 = (s32[1,512]{1,0:T(1,128)S(1)}, s32[1,512]{1,0:T(1,128)}, u32[]{:S(2)}) copy-start(s32[1,512]{1,0:T(1,128)} %param.13) | copy-start | bytes 6148
  28.4 3.3 %collective-permute-start = (bf16[1,2,3,256]{3,2,1,0:T(4,128)(2,1)S(1)}, bf16[1,2,3,256]{3,2,1,0:T(4,128)(2,1)S(1)}, u32[]{:S(2)}, u32[]{:S(2)}) collective-permute-start(bf16[1,2,3,256]{3,2,1,0:T(4,128)(2,1)S(1)} %get-tuple-element.15), channel_id=1, source_target_pairs={{0,1},{1,2},{2,3},{4,5},{5,6},{6,7},{8,9},{9,10},{10,11},{12,13},{... | collective-permute-start | bytes 9224 | tf_op jit(solution)/shard_map/ppermute | solution.py:19
  29.7 4.8 %collective-permute-start.1 = (bf16[1,2,3,256]{3,2,1,0:T(4,128)(2,1)S(1)}, bf16[1,2,3,256]{3,2,1,0:T(4,128)(2,1)S(1)}, u32[]{:S(2)}, u32[]{:S(2)}) collective-permute-start(bf16[1,2,3,256]{3,2,1,0:T(4,128)(2,1)S(1)} %get-tuple-element.16), channel_id=1, source_target_pairs={{1,0},{2,1},{3,2},{5,4},{6,5},{7,6},{9,8},{10,9},{11,10},{13,12},{... | collective-permute-start | bytes 9224 | tf_op jit(solution)/shard_map/ppermute | solution.py:20
  43.9 4.9 %copy-start.10 = (f32[2,32,512]{2,1,0:T(8,128)}, f32[2,32,512]{2,1,0:T(8,128)S(1)}, u32[]{:S(2)}) copy-start(f32[2,32,512]{2,1,0:T(8,128)S(1)} %fusion.30) | copy-start | bytes 393220
  48.7 42.9 %copy-start.2 = (bf16[1,2,128,2048]{3,2,1,0:T(8,128)(2,1)S(1)}, bf16[1,2,128,2048]{3,2,1,0:T(8,128)(2,1)}, u32[]{:S(2)}) copy-start(bf16[1,2,128,2048]{3,2,1,0:T(8,128)(2,1)} %copy-done.1) | copy-start | bytes 3145732
  48.8 5.9 %collective-permute-start.2 = (bf16[1,2,3,256]{3,2,1,0:T(4,128)(2,1)S(1)}, bf16[1,2,3,256]{3,2,1,0:T(4,128)(2,1)S(1)}, u32[]{:S(2)}, u32[]{:S(2)}) collective-permute-start(bf16[1,2,3,256]{3,2,1,0:T(4,128)(2,1)S(1)} %get-tuple-element.13), channel_id=1, source_target_pairs={{0,1},{1,2},{2,3},{4,5},{5,6},{6,7},{8,9},{9,10},{10,11},{12,13},{... | collective-permute-start | bytes 9224 | tf_op jit(solution)/shard_map/ppermute | solution.py:19
  53.2 3.1 %collective-permute-start.3 = (bf16[1,2,3,256]{3,2,1,0:T(4,128)(2,1)S(1)}, bf16[1,2,3,256]{3,2,1,0:T(4,128)(2,1)S(1)}, u32[]{:S(2)}, u32[]{:S(2)}) collective-permute-start(bf16[1,2,3,256]{3,2,1,0:T(4,128)(2,1)S(1)} %get-tuple-element.14), channel_id=1, source_target_pairs={{1,0},{2,1},{3,2},{5,4},{6,5},{7,6},{9,8},{10,9},{11,10},{13,12},{... | collective-permute-start | bytes 9224 | tf_op jit(solution)/shard_map/ppermute | solution.py:20
where the time goes:
time: 93.9 us; the launch traced here: 93.4 us
  blocking collectives  30.8 us (33%)
  other arithmetic  18.3 us (19%)
  matrix products  18.2 us (19%)
  starting transfers between devices  15.5 us (17%)
  waiting for transfers between devices  5.59 us (6%)
  local copies, waits for them, and re-layouts  3.28 us (3%)
  between operations  1.63 us (2%)
    all_gather x1, blocking collectives, local(): lax.all_gather(back_grid, 'facet', axis=0, tiled=True)  30.8 us
    another operation x4, other arithmetic  12.2 us
    dot_general x1, matrix products, visibility_rows(): jnp.einsum('vj,pcj->pcv', degrid_table, grid_values, preferred_element_ty...  9.35 us
    all_to_all x1, starting transfers between devices, local(): lax.all_to_all(contribution, 'facet', split_axis=0, concat_axis=0, tiled=...  7.25 us
    ppermute x2, starting transfers between devices, padded_2(): before = lax.ppermute(last, axis, up)  5.69 us
    dot_general x1, matrix products, visibility_rows(): jnp.einsum('vj,pcv->pcj', degrid_table, residual.astype(jnp.bfloat16), pr...  4.85 us
    convert_element_type x1, other arithmetic, local(): convolve(padded_back, column_kernel, columns, True).astype(jnp.bfloat16)  4.52 us
    ppermute x2, waiting for transfers between devices, padded_2(): after = lax.ppermute(first, axis, down)  4.44 us
  transfers between devices with their start and end apart: 5, of which 3 were waited for; matrix products, arithmetic and copies ran while one was open for 7% of the time, Pallas kernels for 0%

commit v1 on v0

v1 whole, which is shorter than its diff:
```python
import functools
import math

import jax
import jax.numpy as jnp
from jax import lax
from jax.experimental import pallas as pl
from jax.experimental.pallas import tpu as pltpu
from jax.sharding import PartitionSpec as P

XC = 128
SG = 256
LANES = 128
EDGE = 8
NT = (((1,), (1,)), ((), ()))
F32 = jnp.float32
BF16 = jnp.bfloat16


def sine(a):
    square = a * a
    total = jnp.full_like(a, 1.0 / math.factorial(17))
    for order in range(15, 0, -2):
        sign = -1.0 if order % 4 == 3 else 1.0
        total = total * square + sign / math.factorial(order)
    return a * total


def cosine(a):
    square = a * a
    total = jnp.full_like(a, -1.0 / math.factorial(18))
    for order in range(16, -1, -2):
        sign = -1.0 if order % 4 == 2 else 1.0
        total = total * square + sign / math.factorial(order)
    return total


def turn(steps, period):
    steps = jnp.bitwise_and(steps, period - 1)
    steps = jnp.where(steps >= period // 2, steps - period, steps)
    angle = steps.astype(F32) * (2.0 * math.pi / period)
    return cosine(angle), sine(angle)


def iota(shape, dim):
    return lax.broadcasted_iota(jnp.int32, shape, dim)


def kernel(
    facets, bands, offsets, owner, count, rowk, colk, cell, sky_hbm, obs_hbm, wt_hbm,
    res_hbm, dirty,
    sky, obs, wt, obs_halo, wt_halo, taper, shift, windowed, table, total,
    send1, recv1, grid, z, z_halo, residual, send2, recv2,
    local_sem, send_sem1, recv_sem1, send_sem2, recv_sem2, halo_send, halo_recv,
):
    me = lax.axis_index("facet")
    band = lax.axis_index("uv")
    right, left = lax.rem(band + 1, bands), lax.rem(band + bands - 1, bands)
    columns, strip = sky.shape
    slots = facets
    blocks = strip // LANES
    taps = colk.shape[0]
    margin = (taps - 1) // 2
    live_slots = cell.shape[1]

    sky_copy = pltpu.make_async_copy(sky_hbm, sky, local_sem.at[0])
    obs_copy = pltpu.make_async_copy(obs_hbm.at[0], obs, local_sem.at[1])
    wt_copy = pltpu.make_async_copy(wt_hbm.at[0], wt, local_sem.at[2])
    sky_copy.start()
    obs_copy.start()
    wt_copy.start()

    barrier = pltpu.get_barrier_semaphore()

    def greet(d, carry):
        pl.semaphore_signal(
            barrier, inc=1, device_id={"facet": lax.rem(me + d, facets)},
            device_id_type=pl.DeviceIdType.MESH,
        )
        return carry

    lax.fori_loop(1, facets, greet, 0)
    for side in (left, right):
        pl.semaphore_signal(
            barrier, inc=1, device_id={"uv": side}, device_id_type=pl.DeviceIdType.MESH
        )

    def exchange(index, src, dst, side):
        return pltpu.make_async_remote_copy(
            src_ref=src, dst_ref=dst, send_sem=halo_send.at[index],
            recv_sem=halo_recv.at[index], device_id={"uv": side},
            device_id_type=pl.DeviceIdType.MESH,
        )

    def out1(d):
        to = lax.rem(me + d, facets)
        return pltpu.make_async_remote_copy(
            src_ref=send1.at[to], dst_ref=recv1.at[me], send_sem=send_sem1.at[to],
            recv_sem=recv_sem1.at[me], device_id={"facet": to},
            device_id_type=pl.DeviceIdType.MESH,
        )

    def in1(d):
        source = lax.rem(me + facets - d, facets)
        return pltpu.make_async_remote_copy(
            src_ref=send1.at[source], dst_ref=recv1.at[source], send_sem=send_sem1.at[source],
            recv_sem=recv_sem1.at[source], device_id={"facet": source},
            device_id_type=pl.DeviceIdType.MESH,
        )

    def out2(d):
        to = lax.rem(me + d, facets)
        return pltpu.make_async_remote_copy(
            src_ref=send2.at[to], dst_ref=recv2.at[me], send_sem=send_sem2.at[to],
            recv_sem=recv_sem2.at[me], device_id={"facet": to},
            device_id_type=pl.DeviceIdType.MESH,
        )

    def in2(d):
        source = lax.rem(me + facets - d, facets)
        return pltpu.make_async_remote_copy(
            src_ref=send2.at[source], dst_ref=recv2.at[source], send_sem=send_sem2.at[source],
            recv_sem=recv_sem2.at[source], device_id={"facet": source},
            device_id_type=pl.DeviceIdType.MESH,
        )

    def each(action):
        def step(d, carry):
            action(d)
            return carry

        lax.fori_loop(1, facets, step, 0)

    position = iota((1, strip), 1)
    taper[...] = sine((position.astype(F32) + 0.5) * (math.pi / strip)) * (1.0 / math.sqrt(strip))
    offset = jnp.zeros((slots, strip), jnp.int32)
    slot_row = iota((slots, strip), 0)
    for i in range(slots):
        offset = jnp.where(slot_row == i, offsets[owner[i]], offset)
    shift_cos, shift_sin = turn(offset * iota((slots, strip), 1), strip)
    shift[0] = shift_cos
    shift[1] = -shift_sin
    frequency = iota((XC, LANES), 0)
    first = (2 * me + 1) * (strip // facets)
    start = turn(frequency * (iota((XC, LANES), 1) + first), strip)
    step_cos, step_sin = turn(frequency * LANES, strip)
    sky_copy.wait()
    windowed[...] = (sky[...].astype(F32) * taper[...]).astype(BF16).astype(F32)
    total[...] = jnp.zeros_like(total)

    def contribute(block, carry):
        c, s = carry
        upper = jnp.concatenate([c, s], axis=1)
        lower = jnp.concatenate([-s, c], axis=1)
        base = jnp.concatenate([upper, lower], axis=0).astype(BF16)
        table[block] = base
        rows = pl.ds(pl.multiple_of(block * LANES, LANES), LANES)
        piece = windowed[:, rows]
        real, imag = shift[0, :, rows], shift[1, :, rows]
        modulated = jnp.concatenate(
            [
                jnp.concatenate([real[i : i + 1] * piece, imag[i : i + 1] * piece], axis=1)
                for i in range(slots)
            ],
            axis=0,
        ).astype(BF16)
        total[...] += lax.dot_general(modulated, base, NT, preferred_element_type=F32)
        return c * step_cos - s * step_sin, s * step_cos + c * step_sin

    lax.fori_loop(0, blocks, contribute, start)
    send1[...] = total[...].astype(BF16).reshape(send1.shape)

    pl.semaphore_wait(barrier, facets + 1)
    each(lambda d: out1(d).start())
    recv1[me] = send1[me]
    early = [
        exchange(0, obs_hbm.at[0, :, pl.ds(columns - 2 * EDGE, 2 * EDGE)], obs_halo.at[0], right),
        exchange(1, obs_hbm.at[0, :, pl.ds(0, 2 * EDGE)], obs_halo.at[1], left),
        exchange(2, wt_hbm.at[0, pl.ds(columns - EDGE, EDGE)], wt_halo.at[0], right),
        exchange(3, wt_hbm.at[0, pl.ds(0, EDGE)], wt_halo.at[1], left),
    ]
    for copy in early:
        copy.start()

    factor = 1.0 / math.sqrt(facets * XC)
    fine_cos, fine_sin = turn(iota((SG, SG), 0) * iota((SG, SG), 1), SG)
    fine_cos = (fine_cos * factor).astype(BF16)
    fine_sin = (fine_sin * factor).astype(BF16)
    distance = iota((SG, live_slots), 0) - cell[...] + margin
    degrid = jnp.zeros((SG, live_slots), F32)
    for t in range(taps):
        degrid = jnp.where(distance == t, rowk[t], degrid)
    degrid = degrid.astype(BF16)
    grid_cos = jnp.dot(fine_cos, degrid, preferred_element_type=F32)
    grid_sin = jnp.dot(fine_sin, degrid, preferred_element_type=F32)
    grid[0:SG, 0:live_slots] = grid_cos.astype(BF16)
    grid[0:SG, live_slots:] = grid_sin.astype(BF16)
    grid[SG:, 0:live_slots] = (-grid_sin).astype(BF16)
    grid[SG:, live_slots:] = grid_cos.astype(BF16)

    each(lambda d: in1(d).wait_recv())
    blank = jnp.zeros((columns, SG - XC), F32)
    sums = [jnp.zeros((columns, SG), F32), jnp.zeros((columns, SG), F32)]
    for f in range(facets):
        place = (2 * f + 1) * (SG // (2 * facets)) % SG
        arrived = recv1[f].astype(F32)
        for q in range(2):
            wide = jnp.concatenate([arrived[:, q * XC : (q + 1) * XC], blank], axis=1)
            sums[q] = sums[q] + pltpu.roll(wide, place, 1)
    z[...] = jnp.concatenate(sums, axis=1)
    late = [
        exchange(4, z.at[pl.ds(columns - EDGE, EDGE)], z_halo.at[0], right),
        exchange(5, z.at[pl.ds(0, EDGE)], z_halo.at[1], left),
    ]
    for copy in late:
        copy.start()

    obs_copy.wait()
    wt_copy.wait()
    for copy in early:
        copy.wait_recv()
    for copy in late:
        copy.wait_recv()
    rows = columns + 2 * EDGE
    before = jnp.where(band == 0, 0.0, z_halo[0])
    after = jnp.where(band == bands - 1, 0.0, z_halo[1])
    padded = jnp.concatenate([before, z[...], after], axis=0)
    convolved = jnp.zeros_like(padded)
    for t in range(taps):
        convolved = convolved + colk[t] * pltpu.roll(padded, (margin - t) % rows, 0)
    model = jnp.dot(convolved.astype(BF16), grid[...], preferred_element_type=F32)
    row = iota((rows, live_slots), 0)
    lowest = jnp.where(band == 0, EDGE, EDGE - margin)
    highest = jnp.where(band == bands - 1, EDGE + columns, EDGE + columns + margin)
    valid = (row >= lowest) & (row < highest) & (iota((rows, live_slots), 1) < count[0])
    weight = jnp.where(valid, jnp.concatenate([wt_halo[0], wt[...], wt_halo[1]], axis=0), 0.0)
    parts = []
    for p in range(2):
        seen = jnp.concatenate(
            [
                obs_halo[0, p].astype(F32)[EDGE:],
                obs[p].astype(F32),
                obs_halo[1, p].astype(F32)[:EDGE],
            ],
            axis=0,
        )
        parts.append(weight * (seen - model[:, p * live_slots : (p + 1) * live_slots]))
        residual[p] = parts[p][EDGE : EDGE + columns]
    res_copy = pltpu.make_async_copy(residual, res_hbm.at[0], local_sem.at[3])
    res_copy.start()
    rounded = jnp.concatenate(parts, axis=1).astype(BF16)
    gridded = lax.dot_general(rounded, grid[...], NT, preferred_element_type=F32)
    back = jnp.zeros_like(gridded)
    for t in range(taps):
        back = back + colk[t] * pltpu.roll(gridded, (t - margin) % rows, 0)
    back = back[EDGE : EDGE + columns]
    for f in range(facets):
        place = (2 * f + 1) * (SG // (2 * facets)) % SG
        send2[f] = jnp.concatenate(
            [
                pltpu.roll(back[:, p * SG : (p + 1) * SG], (SG - place) % SG, 1)[:, :XC]
                for p in range(2)
            ],
            axis=1,
        ).astype(BF16)
    each(lambda d: out2(d).start())
    recv2[me] = send2[me]
    for copy in early + late:
        copy.wait_send()
    each(lambda d: out1(d).wait_send())
    each(lambda d: in2(d).wait_recv())

    pieces = recv2[...].reshape(slots * columns, 2 * XC)

    def image(block, carry):
        rows = pl.ds(pl.multiple_of(block * LANES, LANES), LANES)
        back_rows = jnp.dot(pieces, table[block], preferred_element_type=F32)
        real, imag = shift[0, :, rows], shift[1, :, rows]
        strip_sum = jnp.zeros((columns, LANES), F32)
        for i in range(slots):
            own = back_rows[i * columns : (i + 1) * columns]
            strip_sum = strip_sum + real[i : i + 1] * own[:, :LANES] + imag[i : i + 1] * own[:, LANES:]
        dirty[:, rows] = strip_sum * taper[:, rows]
        return carry

    lax.fori_loop(0, blocks, image, 0)
    res_copy.wait()
    each(lambda d: out2(d).wait_send())


def local(
    sky_image, subgrid_offsets, owner_order, visibility_count, visibility_cell, observed,
    visibility_weight, row_kernel, column_kernel,
):
    facets, bands = lax.axis_size("facet"), lax.axis_size("uv")
    columns, strip = sky_image.shape
    slots = facets
    live_slots = visibility_cell.shape[1]
    smem, vmem = pl.BlockSpec(memory_space=pltpu.SMEM), pl.BlockSpec(memory_space=pltpu.VMEM)
    hbm = pl.BlockSpec(memory_space=pl.ANY)
    dma = pltpu.SemaphoreType.DMA
    traded = pltpu.VMEM((facets, columns, 2 * XC), BF16)
    return pl.pallas_call(
        functools.partial(kernel, facets, bands),
        out_shape=(
            jax.ShapeDtypeStruct(observed.shape, F32),
            jax.ShapeDtypeStruct(sky_image.shape, F32),
        ),
        in_specs=[smem, smem, smem, smem, smem, vmem, hbm, hbm, hbm],
        out_specs=(hbm, vmem),
        scratch_shapes=[
            pltpu.VMEM((columns, strip), BF16),
            pltpu.VMEM((2, columns, live_slots), BF16),
            pltpu.VMEM((columns, live_slots), F32),
            pltpu.VMEM((2, 2, 2 * EDGE, live_slots), BF16),
            pltpu.VMEM((2, EDGE, live_slots), F32),
            pltpu.VMEM((1, strip), F32),
            pltpu.VMEM((2, slots, strip), F32),
            pltpu.VMEM((columns, strip), F32),
            pltpu.VMEM((strip // LANES, 2 * XC, 2 * LANES), BF16),
            pltpu.VMEM((slots * columns, 2 * XC), F32),
            traded,
            traded,
            pltpu.VMEM((2 * SG, 2 * live_slots), BF16),
            pltpu.VMEM((columns, 2 * SG), F32),
            pltpu.VMEM((2, EDGE, 2 * SG), F32),
            pltpu.VMEM((2, columns, live_slots), F32),
            traded,
            traded,
            dma((4,)),
            dma((facets,)),
            dma((facets,)),
            dma((facets,)),
            dma((facets,)),
            dma((6,)),
            dma((6,)),
        ],
        compiler_params=pltpu.CompilerParams(
            collective_id=0, has_side_effects=True, vmem_limit_bytes=32 * 1024 * 1024
        ),
    )(
        subgrid_offsets, owner_order, visibility_count, row_kernel, column_kernel,
        visibility_cell, sky_image, observed, visibility_weight,
    )


def solution(mesh):
    in_specs = (
        P("uv", "facet"), P(), P(), P("facet"), P("facet", None), P("facet", None, "uv", None),
        P("facet", "uv", None), P(), P(),
    )
    out_specs = (P("facet", None, "uv", None), P("uv", "facet"))
    return jax.shard_map(local, mesh=mesh, in_specs=in_specs, out_specs=out_specs, check_vma=False)
```

time: 93.9 us -> 31.1 us (0.33)
  the two profiles are of different devices: /device:TPU:0 before, /device:TPU:1 now
where the time goes in v1:
time: 31.1 us; the launch traced here: 30.5 us
  Pallas kernels  23.9 us (77%)
  local copies, waits for them, and re-layouts  5.28 us (17%)
  between operations  1.37 us (4%)
    pallas_call x1, Pallas kernels, local(): pl.pallas_call(functools.partial(kernel, facets, bands), out_shape=(jax.S...  23.9 us
    unnamed x18, local copies, waits for them, and re-layouts  5.28 us

profile of v1, /device:TPU:1, one launch (start us, length us, event | category | flops | bytes accessed | tf_op | source)
XLA Modules:
  0.0 30.5 jit_solution(9026383797226207567)
XLA Ops:
  0.6 0.0 copy-start.6
  0.6 0.0 copy-start.5
  0.7 0.0 copy-start.4
  1.3 0.0 copy-done.6
  1.3 0.0 copy-done.5
  1.4 0.0 copy-done.4
  1.4 0.0 copy-start
  1.4 0.9 %copy-done = bf16[32,2048]{1,0:T(8,128)(2,1)S(1)} copy-done((bf16[32,2048]{1,0:T(8,128)(2,1)S(1)}, bf16[32,2048]{1,0:T(8,128)(2,1)}, u32[]{:S(2)}) %copy-start) | copy-done | bytes 131096
  2.3 0.0 copy-start.1
  2.3 0.8 %copy-done.1 = bf16[1,2,32,512]{3,2,1,0:T(8,128)(2,1)S(1)} copy-done((bf16[1,2,32,512]{3,2,1,0:T(8,128)(2,1)S(1)}, bf16[1,2,32,512]{3,2,1,0:T(8,128)(2,1)}, u32[]{:S(2)}) %copy-start.1) | copy-done | bytes 65560
  3.1 0.0 copy-start.2
  3.1 0.8 %copy-done.2 = f32[1,32,512]{2,1,0:T(8,128)S(1)} copy-done((f32[1,32,512]{2,1,0:T(8,128)S(1)}, f32[1,32,512]{2,1,0:T(8,128)}, u32[]{:S(2)}) %copy-start.2) | copy-done | bytes 65560
  3.9 0.0 copy-start.3
  4.0 0.7 %copy-done.3 = s32[1,512]{1,0:T(1,128)S(1)} copy-done((s32[1,512]{1,0:T(1,128)S(1)}, s32[1,512]{1,0:T(1,128)}, u32[]{:S(2)}) %copy-start.3) | copy-done | bytes 2072
  4.6 0.0 copy-start.7
  4.6 0.7 %copy-done.7 = f32[7]{0:T(128)S(1)} copy-done((f32[7]{0:T(128)S(1)}, f32[7]{0:T(128)}, u32[]{:S(2)}) %copy-start.7) | copy-done | bytes 52
  5.3 23.9 %shard_map.104 = (f32[1,2,32,512]{3,2,1,0:T(8,128)S(1)}, f32[32,2048]{1,0:T(8,128)S(1)}) custom-call(s32[8]{0:T(128)S(1)} %copy-done.4, s32[8]{0:T(128)S(1)} %copy-done.5, s32[1]{0:T(128)S(6)} %copy.13.count, f32[7]{0:T(128)S(1)} %copy-done.6, f32[7]{0:T(128)S(1)} %copy-done.7, s32[1,512]{1,0:T(1,128)S(1)} %copy-done.3, bf16[32,2048]{1,0:T(8,128)(2,1)S(1)} %copy-done, ...), custom_call_target="tpu_custom_call" | custom-call | tf_op jit(solution)/shard_map/pallas_call | solution.py:303
  29.2 0.7 %copy.14 = f32[1,2,32,512]{3,2,1,0:T(8,128)} copy(f32[1,2,32,512]{3,2,1,0:T(8,128)S(1)} %get-tuple-element.4) | data formatting | bytes 262144
  29.8 0.7 %copy.15 = f32[32,2048]{1,0:T(8,128)} copy(f32[32,2048]{1,0:T(8,128)S(1)} %get-tuple-element.5) | data formatting | bytes 524288
Async XLA Ops:
  0.6 0.7 %copy-start.6 = (f32[7]{0:T(128)S(1)}, f32[7]{0:T(128)}, u32[]{:S(2)}) copy-start(f32[7]{0:T(128)} %rowk.1) | copy-start | bytes 88
  0.6 0.7 %copy-start.5 = (s32[8]{0:T(128)S(1)}, s32[8]{0:T(128)}, u32[]{:S(2)}) copy-start(s32[8]{0:T(128)} %owner.1) | copy-start | bytes 100
  0.7 0.7 %copy-start.4 = (s32[8]{0:T(128)S(1)}, s32[8]{0:T(128)}, u32[]{:S(2)}) copy-start(s32[8]{0:T(128)} %offsets.1) | copy-start | bytes 100
  1.4 0.9 %copy-start = (bf16[32,2048]{1,0:T(8,128)(2,1)S(1)}, bf16[32,2048]{1,0:T(8,128)(2,1)}, u32[]{:S(2)}) copy-start(bf16[32,2048]{1,0:T(8,128)(2,1)} %sky_hbm.1) | copy-start | bytes 393220
  2.3 0.8 %copy-start.1 = (bf16[1,2,32,512]{3,2,1,0:T(8,128)(2,1)S(1)}, bf16[1,2,32,512]{3,2,1,0:T(8,128)(2,1)}, u32[]{:S(2)}) copy-start(bf16[1,2,32,512]{3,2,1,0:T(8,128)(2,1)} %obs_hbm.1) | copy-start | bytes 196612
  3.1 0.8 %copy-start.2 = (f32[1,32,512]{2,1,0:T(8,128)S(1)}, f32[1,32,512]{2,1,0:T(8,128)}, u32[]{:S(2)}) copy-start(f32[1,32,512]{2,1,0:T(8,128)} %wt_hbm.1) | copy-start | bytes 196612
  3.9 0.7 %copy-start.3 = (s32[1,512]{1,0:T(1,128)S(1)}, s32[1,512]{1,0:T(1,128)}, u32[]{:S(2)}) copy-start(s32[1,512]{1,0:T(1,128)} %cell.1) | copy-start | bytes 6148
  4.6 0.7 %copy-start.7 = (f32[7]{0:T(128)S(1)}, f32[7]{0:T(128)}, u32[]{:S(2)}) copy-start(f32[7]{0:T(128)} %colk.1) | copy-start | bytes 88

commit v2 on v1

--- a/solution.py
+++ b/solution.py
@@ -12,6 +12,7 @@
 SG = 256
 LANES = 128
 EDGE = 8
+GROUP = 4
 NT = (((1,), (1,)), ((), ()))
 F32 = jnp.float32
 BF16 = jnp.bfloat16
@@ -47,9 +48,10 @@
 
 
 def kernel(
-    facets, bands, offsets, owner, count, rowk, colk, cell, sky_hbm, obs_hbm, wt_hbm,
+    facets, bands, offsets_hbm, owner_hbm, count_hbm, rowk_hbm, colk_hbm, cell_hbm,
+    sky_hbm, obs_hbm, wt_hbm,
     res_hbm, dirty,
-    sky, obs, wt, obs_halo, wt_halo, taper, shift, windowed, table, total,
+    offsets, owner, count, rowk, colk, cell, sky, obs, wt, obs_halo, wt_halo, taper, shift, windowed, table, total,
     send1, recv1, grid, z, z_halo, residual, send2, recv2,
     local_sem, send_sem1, recv_sem1, send_sem2, recv_sem2, halo_send, halo_recv,
 ):
@@ -66,7 +68,18 @@
     sky_copy = pltpu.make_async_copy(sky_hbm, sky, local_sem.at[0])
     obs_copy = pltpu.make_async_copy(obs_hbm.at[0], obs, local_sem.at[1])
     wt_copy = pltpu.make_async_copy(wt_hbm.at[0], wt, local_sem.at[2])
+    small = [
+        pltpu.make_async_copy(source, target, local_sem.at[4 + i])
+        for i, (source, target) in enumerate(
+            [
+                (offsets_hbm, offsets), (owner_hbm, owner), (count_hbm, count),
+                (rowk_hbm, rowk), (colk_hbm, colk), (cell_hbm, cell),
+            ]
+        )
+    ]
     sky_copy.start()
+    for copy in small:
+        copy.start()
     obs_copy.start()
     wt_copy.start()
 
@@ -133,6 +146,12 @@
 
     position = iota((1, strip), 1)
     taper[...] = sine((position.astype(F32) + 0.5) * (math.pi / strip)) * (1.0 / math.sqrt(strip))
+    frequency = iota((XC, LANES), 0)
+    first = (2 * me + 1) * (strip // facets)
+    start = turn(frequency * (iota((XC, LANES), 1) + first), strip)
+    step_cos, step_sin = turn(frequency * LANES, strip)
+    for copy in small:
+        copy.wait()
     offset = jnp.zeros((slots, strip), jnp.int32)
     slot_row = iota((slots, strip), 0)
     for i in range(slots):
@@ -140,34 +159,42 @@
     shift_cos, shift_sin = turn(offset * iota((slots, strip), 1), strip)
     shift[0] = shift_cos
     shift[1] = -shift_sin
-    frequency = iota((XC, LANES), 0)
-    first = (2 * me + 1) * (strip // facets)
-    start = turn(frequency * (iota((XC, LANES), 1) + first), strip)
-    step_cos, step_sin = turn(frequency * LANES, strip)
     sky_copy.wait()
     windowed[...] = (sky[...].astype(F32) * taper[...]).astype(BF16).astype(F32)
     total[...] = jnp.zeros_like(total)
 
-    def contribute(block, carry):
+    def contribute(group, carry):
         c, s = carry
-        upper = jnp.concatenate([c, s], axis=1)
-        lower = jnp.concatenate([-s, c], axis=1)
-        base = jnp.concatenate([upper, lower], axis=0).astype(BF16)
-        table[block] = base
-        rows = pl.ds(pl.multiple_of(block * LANES, LANES), LANES)
-        piece = windowed[:, rows]
-        real, imag = shift[0, :, rows], shift[1, :, rows]
-        modulated = jnp.concatenate(
-            [
-                jnp.concatenate([real[i : i + 1] * piece, imag[i : i + 1] * piece], axis=1)
-                for i in range(slots)
-            ],
-            axis=0,
-        ).astype(BF16)
-        total[...] += lax.dot_general(modulated, base, NT, preferred_element_type=F32)
-        return c * step_cos - s * step_sin, s * step_cos + c * step_sin
-
-    lax.fori_loop(0, blocks, contribute, start)
+        bases, pieces = [], []
+        for member in range(GROUP):
+            block = group * GROUP + member
+            upper = jnp.concatenate([c, s], axis=1)
+            lower = jnp.concatenate([-s, c], axis=1)
+            base = jnp.concatenate([upper, lower], axis=0).astype(BF16)
+            table[block] = base
+            bases.append(base)
+            rows = pl.ds(pl.multiple_of(block * LANES, LANES), LANES)
+            piece = windowed[:, rows]
+            real, imag = shift[0, :, rows], shift[1, :, rows]
+            pieces.append(
+                jnp.concatenate(
+                    [
+                        jnp.concatenate(
+                            [real[i : i + 1] * piece, imag[i : i + 1] * piece], axis=1
+                        ).astype(BF16)
+                        for i in range(slots)
+                    ],
+                    axis=0,
+                )
+            )
+            c, s = c * step_cos - s * step_sin, s * step_cos + c * step_sin
+        total[...] += lax.dot_general(
+            jnp.concatenate(pieces, axis=1), jnp.concatenate(bases, axis=1), NT,
+            preferred_element_type=F32,
+        )
+        return c, s
+
+    lax.fori_loop(0, blocks // GROUP, contribute, start)
     send1[...] = total[...].astype(BF16).reshape(send1.shape)
 
     pl.semaphore_wait(barrier, facets + 1)
@@ -283,7 +310,7 @@
         dirty[:, rows] = strip_sum * taper[:, rows]
         return carry
 
-    lax.fori_loop(0, blocks, image, 0)
+    lax.fori_loop(0, blocks, image, 0, unroll=GROUP)
     res_copy.wait()
     each(lambda d: out2(d).wait_send())
 
@@ -296,8 +323,8 @@
     columns, strip = sky_image.shape
     slots = facets
     live_slots = visibility_cell.shape[1]
-    smem, vmem = pl.BlockSpec(memory_space=pltpu.SMEM), pl.BlockSpec(memory_space=pltpu.VMEM)
-    hbm = pl.BlockSpec(memory_space=pl.ANY)
+    vmem = pl.BlockSpec(memory_space=pltpu.VMEM)
+    hbm = pl.BlockSpec(memory_space=pltpu.HBM)
     dma = pltpu.SemaphoreType.DMA
     traded = pltpu.VMEM((facets, columns, 2 * XC), BF16)
     return pl.pallas_call(
@@ -306,9 +333,15 @@
             jax.ShapeDtypeStruct(observed.shape, F32),
             jax.ShapeDtypeStruct(sky_image.shape, F32),
         ),
-        in_specs=[smem, smem, smem, smem, smem, vmem, hbm, hbm, hbm],
+        in_specs=[hbm] * 9,
         out_specs=(hbm, vmem),
         scratch_shapes=[
+            pltpu.SMEM(subgrid_offsets.shape, jnp.int32),
+            pltpu.SMEM(owner_order.shape, jnp.int32),
+            pltpu.SMEM(visibility_count.shape, jnp.int32),
+            pltpu.SMEM(row_kernel.shape, F32),
+            pltpu.SMEM(column_kernel.shape, F32),
+            pltpu.VMEM(visibility_cell.shape, jnp.int32),
             pltpu.VMEM((columns, strip), BF16),
             pltpu.VMEM((2, columns, live_slots), BF16),
             pltpu.VMEM((columns, live_slots), F32),
@@ -327,7 +360,7 @@
             pltpu.VMEM((2, columns, live_slots), F32),
             traded,
             traded,
-            dma((4,)),
+            dma((10,)),
             dma((facets,)),
             dma((facets,)),
             dma((facets,)),
@@ -336,7 +369,7 @@
             dma((6,)),
         ],
         compiler_params=pltpu.CompilerParams(
-            collective_id=0, has_side_effects=True, vmem_limit_bytes=32 * 1024 * 1024
+            collective_id=0, has_side_effects=True, vmem_limit_bytes=63 * 1024 * 1024
         ),
     )(
         subgrid_offsets, owner_order, visibility_count, row_kernel, column_kernel,

time: 31.1 us -> 24.1 us (0.77); the launches traced: 30.5 us -> 24 us
  Pallas kernels: 23.9 us -> 20.4 us
  local copies, waits for them, and re-layouts: 5.28 us -> 2.32 us
    pallas_call x1, Pallas kernels: 23.9 us -> 20.4 us  [local(): pl.pallas_call(functools.partial(kernel, facets, bands), out_shape=(jax.S...]
    unnamed x18 -> x4, local copies, waits for them, and re-layouts: 5.28 us -> 2.32 us
where the time goes in v2:
time: 24.1 us; the launch traced here: 24 us
  Pallas kernels  20.4 us (85%)
  local copies, waits for them, and re-layouts  2.32 us (10%)
  between operations  1.29 us (5%)
    pallas_call x1, Pallas kernels, local(): pl.pallas_call(functools.partial(kernel, facets, bands), out_shape=(jax.S...  20.4 us
    unnamed x4, local copies, waits for them, and re-layouts  2.32 us

profile of v2, /device:TPU:1, one launch (start us, length us, event | category | flops | bytes accessed | tf_op | source)
XLA Modules:
  0.0 24.0 jit_solution(11330818108438990283)
XLA Ops:
  1.3 20.4 %shard_map.104 = (f32[1,2,32,512]{3,2,1,0:T(8,128)}, f32[32,2048]{1,0:T(8,128)}) custom-call(s32[8]{0:T(128)} %offsets_hbm.1, s32[8]{0:T(128)} %owner_hbm.1, s32[1]{0:T(128)S(6)} %copy.13.count_hbm, f32[7]{0:T(128)} %rowk_hbm.1, f32[7]{0:T(128)} %colk_hbm.1, s32[1,512]{1,0:T(1,128)} %cell_hbm.1, bf16[32,2048]{1,0:T(8,128)(2,1)} %sky_hbm.1, ...), custom_call_target="tpu_custom_call" | custom-call | tf_op jit(solution)/shard_map/pallas_call | solution.py:330
  21.6 0.0 copy-start
  21.7 1.6 %copy.14 = f32[1,2,32,512]{3,2,1,0:T(8,128)} copy(f32[1,2,32,512]{3,2,1,0:T(8,128)} %get-tuple-element.4) | data formatting | bytes 262144
  23.3 0.0 copy-done
  23.3 0.7 %copy.15 = f32[32,2048]{1,0:T(8,128)} copy(f32[32,2048]{1,0:T(8,128)S(1)} %copy-done) | data formatting | bytes 524288
Async XLA Ops:
  21.6 1.6 %copy-start = (f32[32,2048]{1,0:T(8,128)S(1)}, f32[32,2048]{1,0:T(8,128)}, u32[]{:S(2)}) copy-start(f32[32,2048]{1,0:T(8,128)} %get-tuple-element.5) | copy-start | bytes 786436

commit v3 on v2

--- a/solution.py
+++ b/solution.py
@@ -50,9 +50,9 @@
 def kernel(
     facets, bands, offsets_hbm, owner_hbm, count_hbm, rowk_hbm, colk_hbm, cell_hbm,
     sky_hbm, obs_hbm, wt_hbm,
-    res_hbm, dirty,
-    offsets, owner, count, rowk, colk, cell, sky, obs, wt, obs_halo, wt_halo, taper, shift, windowed, table, total,
-    send1, recv1, grid, z, z_halo, residual, send2, recv2,
+    residual, collected, table, shift, taper,
+    offsets, owner, count, rowk, colk, cell, sky, obs, wt, obs_halo, wt_halo, windowed, total,
+    send1, recv1, grid, z, z_halo, send2, recv2,
     local_sem, send_sem1, recv_sem1, send_sem2, recv_sem2, halo_send, halo_recv,
 ):
     me = lax.axis_index("facet")
@@ -272,9 +272,7 @@
             axis=0,
         )
         parts.append(weight * (seen - model[:, p * live_slots : (p + 1) * live_slots]))
-        residual[p] = parts[p][EDGE : EDGE + columns]
-    res_copy = pltpu.make_async_copy(residual, res_hbm.at[0], local_sem.at[3])
-    res_copy.start()
+        residual[0, p] = parts[p][EDGE : EDGE + columns]
     rounded = jnp.concatenate(parts, axis=1).astype(BF16)
     gridded = lax.dot_general(rounded, grid[...], NT, preferred_element_type=F32)
     back = jnp.zeros_like(gridded)
@@ -297,22 +295,41 @@
     each(lambda d: out1(d).wait_send())
     each(lambda d: in2(d).wait_recv())
 
-    pieces = recv2[...].reshape(slots * columns, 2 * XC)
-
-    def image(block, carry):
-        rows = pl.ds(pl.multiple_of(block * LANES, LANES), LANES)
-        back_rows = jnp.dot(pieces, table[block], preferred_element_type=F32)
-        real, imag = shift[0, :, rows], shift[1, :, rows]
-        strip_sum = jnp.zeros((columns, LANES), F32)
-        for i in range(slots):
-            own = back_rows[i * columns : (i + 1) * columns]
-            strip_sum = strip_sum + real[i : i + 1] * own[:, :LANES] + imag[i : i + 1] * own[:, LANES:]
-        dirty[:, rows] = strip_sum * taper[:, rows]
-        return carry
-
-    lax.fori_loop(0, blocks, image, 0, unroll=GROUP)
-    res_copy.wait()
+    collected[...] = recv2[...]
     each(lambda d: out2(d).wait_send())
+
+
+def image_kernel(
+    residual, collected, table, shift, taper, residual_hbm, dirty_hbm, dirty, sem
+):
+    slots, columns = collected.shape[:2]
+    strip = taper.shape[1]
+    groups = strip // LANES // GROUP
+    residual_copy = pltpu.make_async_copy(residual, residual_hbm, sem.at[groups])
+    residual_copy.start()
+    pieces = collected[...].reshape(slots * columns, 2 * XC)
+    copies = []
+    for group in range(groups):
+        for block in range(group * GROUP, (group + 1) * GROUP):
+            rows = slice(block * LANES, (block + 1) * LANES)
+            back_rows = jnp.dot(pieces, table[block], preferred_element_type=F32)
+            real, imag = shift[0, :, rows], shift[1, :, rows]
+            strip_sum = jnp.zeros((columns, LANES), F32)
+            for i in range(slots):
+                own = back_rows[i * columns : (i + 1) * columns]
+                strip_sum = strip_sum + real[i : i + 1] * own[:, :LANES]
+                strip_sum = strip_sum + imag[i : i + 1] * own[:, LANES:]
+            dirty[:, rows] = strip_sum * taper[:, rows]
+        rows = pl.ds(group * GROUP * LANES, GROUP * LANES)
+        copies.append(pltpu.make_async_copy(dirty.at[:, rows], dirty_hbm.at[:, rows], sem.at[group]))
+        copies[-1].start()
+    for copy in copies:
+        copy.wait()
+    residual_copy.wait()
+
+
+def pin(operand):
+    return pltpu.with_memory_space_constraint(operand, pltpu.HBM)
 
 
 def local(
@@ -327,14 +344,17 @@
     hbm = pl.BlockSpec(memory_space=pltpu.HBM)
     dma = pltpu.SemaphoreType.DMA
     traded = pltpu.VMEM((facets, columns, 2 * XC), BF16)
-    return pl.pallas_call(
+    kept = pl.pallas_call(
         functools.partial(kernel, facets, bands),
         out_shape=(
-            jax.ShapeDtypeStruct(observed.shape, F32),
-            jax.ShapeDtypeStruct(sky_image.shape, F32),
+            pltpu.VMEM(observed.shape, F32),
+            pltpu.VMEM((facets, columns, 2 * XC), BF16),
+            pltpu.VMEM((strip // LANES, 2 * XC, 2 * LANES), BF16),
+            pltpu.VMEM((2, slots, strip), F32),
+            pltpu.VMEM((1, strip), F32),
         ),
         in_specs=[hbm] * 9,
-        out_specs=(hbm, vmem),
+        out_specs=(vmem,) * 5,
         scratch_shapes=[
             pltpu.SMEM(subgrid_offsets.shape, jnp.int32),
             pltpu.SMEM(owner_order.shape, jnp.int32),
@@ -347,17 +367,13 @@
             pltpu.VMEM((columns, live_slots), F32),
             pltpu.VMEM((2, 2, 2 * EDGE, live_slots), BF16),
             pltpu.VMEM((2, EDGE, live_slots), F32),
-            pltpu.VMEM((1, strip), F32),
-            pltpu.VMEM((2, slots, strip), F32),
             pltpu.VMEM((columns, strip), F32),
-            pltpu.VMEM((strip // LANES, 2 * XC, 2 * LANES), BF16),
             pltpu.VMEM((slots * columns, 2 * XC), F32),
             traded,
             traded,
             pltpu.VMEM((2 * SG, 2 * live_slots), BF16),
             pltpu.VMEM((columns, 2 * SG), F32),
             pltpu.VMEM((2, EDGE, 2 * SG), F32),
-            pltpu.VMEM((2, columns, live_slots), F32),
             traded,
             traded,
             dma((10,)),
@@ -369,12 +385,27 @@
             dma((6,)),
         ],
         compiler_params=pltpu.CompilerParams(
-            collective_id=0, has_side_effects=True, vmem_limit_bytes=63 * 1024 * 1024
+            collective_id=0, has_side_effects=True, vmem_limit_bytes=32 * 1024 * 1024
         ),
     )(
-        subgrid_offsets, owner_order, visibility_count, row_kernel, column_kernel,
-        visibility_cell, sky_image, observed, visibility_weight,
+        pin(subgrid_offsets), pin(owner_order), visibility_count, pin(row_kernel),
+        pin(column_kernel), pin(visibility_cell), pin(sky_image), pin(observed),
+        pin(visibility_weight),
     )
+    return pl.pallas_call(
+        image_kernel,
+        out_shape=(
+            jax.ShapeDtypeStruct(observed.shape, F32),
+            jax.ShapeDtypeStruct(sky_image.shape, F32),
+        ),
+        in_specs=[vmem] * 5,
+        out_specs=(hbm, hbm),
+        scratch_shapes=[
+            pltpu.VMEM((columns, strip), F32),
+            dma((strip // LANES // GROUP + 1,)),
+        ],
+        compiler_params=pltpu.CompilerParams(vmem_limit_bytes=32 * 1024 * 1024),
+    )(*kept)
 
 
 def solution(mesh):

time: 24.1 us -> 21.3 us (0.88)
  local copies, waits for them, and re-layouts: 2.32 us -> 0 us
  Pallas kernels: 20.4 us -> 19.8 us
    unnamed x4 -> x0, local copies, waits for them, and re-layouts: 2.32 us -> none
    pallas_call x1 -> x2, Pallas kernels: 20.4 us -> 19.8 us  [the longest x1 18.4 us: local(): pl.pallas_call(functools.partial(kernel, facets, bands), out_shape=(pltpu...]
where the time goes in v3:
time: 21.3 us; the launch traced here: 21.1 us
  Pallas kernels  19.8 us (93%)
  between operations  1.29 us (6%)
    pallas_call x1, Pallas kernels, local(): pl.pallas_call(functools.partial(kernel, facets, bands), out_shape=(pltpu...  18.4 us
    pallas_call x1, Pallas kernels, local(): pl.pallas_call(image_kernel, out_shape=(jax.ShapeDtypeStruct(observed.sha...  1.39 us

profile of v3, /device:TPU:1, one launch (start us, length us, event | category | flops | bytes accessed | tf_op | source)
XLA Modules:
  0.0 21.1 jit_solution(18183998304429616488)
XLA Ops:
  1.3 18.4 %shard_map.104 = (f32[1,2,32,512]{3,2,1,0:T(8,128)S(1)}, bf16[8,32,256]{2,1,0:T(8,128)(2,1)S(1)}, bf16[16,256,256]{2,1,0:T(8,128)(2,1)S(1)}, f32[2,8,2048]{2,1,0:T(8,128)S(1)}, f32[1,2048]{1,0:T(1,128)S(1)}) custom-call(s32[8]{0:T(128)} %offsets_hbm.1, s32[8]{0:T(128)} %owner_hbm.1, s32[1]{0:T(128)S(6)} %copy.11.count_hbm, f32[7]{0:T(128)} %rowk_hbm.1, ...), custom_call_target="tpu_custom_call" | custom-call | tf_op jit(solution)/shard_map/pallas_call | solution.py:347
  19.7 1.4 %shard_map.105 = (f32[1,2,32,512]{3,2,1,0:T(8,128)}, f32[32,2048]{1,0:T(8,128)}) custom-call(f32[1,2,32,512]{3,2,1,0:T(8,128)S(1)} %get-tuple-element.7.residual, bf16[8,32,256]{2,1,0:T(8,128)(2,1)S(1)} %get-tuple-element.8.collected, bf16[16,256,256]{2,1,0:T(8,128)(2,1)S(1)} %get-tuple-element.9.table, f32[2,8,2048]{2,1,0:T(8,128)S(1)} %get-tuple-element.10.shift, ...), custom_call_target="tpu_custom_call" | custom-call | tf_op jit(solution)/shard_map/pallas_call | solution.py:395

commit v4 on v3

--- a/solution.py
+++ b/solution.py
@@ -13,7 +13,6 @@
 LANES = 128
 EDGE = 8
 GROUP = 4
-NT = (((1,), (1,)), ((), ()))
 F32 = jnp.float32
 BF16 = jnp.bfloat16
 
@@ -51,8 +50,8 @@
     facets, bands, offsets_hbm, owner_hbm, count_hbm, rowk_hbm, colk_hbm, cell_hbm,
     sky_hbm, obs_hbm, wt_hbm,
     residual, collected, table, shift, taper,
-    offsets, owner, count, rowk, colk, cell, sky, obs, wt, obs_halo, wt_halo, windowed, total,
-    send1, recv1, grid, z, z_halo, send2, recv2,
+    offsets, owner, count, rowk, colk, cell, sky, obs, wt, obs_halo, wt_halo, windowed, across,
+    send1, recv1, grid, back_table, z, z_halo, send2, recv2,
     local_sem, send_sem1, recv_sem1, send_sem2, recv_sem2, halo_send, halo_recv,
 ):
     me = lax.axis_index("facet")
@@ -105,101 +104,104 @@
             device_id_type=pl.DeviceIdType.MESH,
         )
 
-    def out1(d):
-        to = lax.rem(me + d, facets)
+    half = facets // 2
+    high, low = me // half, lax.rem(me, half)
+
+    def peer(d):
+        return lax.rem(high + d // half, 2) * half + lax.rem(low + d % half, half)
+
+    def opposite(d):
+        return d // half * half + (half - d % half) % half
+
+    def send_contribution(d):
         return pltpu.make_async_remote_copy(
-            src_ref=send1.at[to], dst_ref=recv1.at[me], send_sem=send_sem1.at[to],
-            recv_sem=recv_sem1.at[me], device_id={"facet": to},
-            device_id_type=pl.DeviceIdType.MESH,
-        )
-
-    def in1(d):
-        source = lax.rem(me + facets - d, facets)
+            src_ref=send1.at[d], dst_ref=recv1.at[me], send_sem=send_sem1.at[d],
+            recv_sem=recv_sem1.at[opposite(d)], device_id={"facet": peer(d)},
+            device_id_type=pl.DeviceIdType.MESH,
+        )
+
+    def take_contribution(d):
         return pltpu.make_async_remote_copy(
-            src_ref=send1.at[source], dst_ref=recv1.at[source], send_sem=send_sem1.at[source],
-            recv_sem=recv_sem1.at[source], device_id={"facet": source},
-            device_id_type=pl.DeviceIdType.MESH,
-        )
-
-    def out2(d):
-        to = lax.rem(me + d, facets)
+            src_ref=send1.at[d], dst_ref=recv1.at[peer(d)], send_sem=send_sem1.at[d],
+            recv_sem=recv_sem1.at[d], device_id={"facet": peer(d)},
+            device_id_type=pl.DeviceIdType.MESH,
+        )
+
+    def send_pieces(d):
         return pltpu.make_async_remote_copy(
-            src_ref=send2.at[to], dst_ref=recv2.at[me], send_sem=send_sem2.at[to],
-            recv_sem=recv_sem2.at[me], device_id={"facet": to},
-            device_id_type=pl.DeviceIdType.MESH,
-        )
-
-    def in2(d):
-        source = lax.rem(me + facets - d, facets)
+            src_ref=send2.at[peer(d)], dst_ref=recv2.at[opposite(d)], send_sem=send_sem2.at[d],
+            recv_sem=recv_sem2.at[opposite(d)], device_id={"facet": peer(d)},
+            device_id_type=pl.DeviceIdType.MESH,
+        )
+
+    def take_pieces(d):
         return pltpu.make_async_remote_copy(
-            src_ref=send2.at[source], dst_ref=recv2.at[source], send_sem=send_sem2.at[source],
-            recv_sem=recv_sem2.at[source], device_id={"facet": source},
-            device_id_type=pl.DeviceIdType.MESH,
-        )
-
-    def each(action):
-        def step(d, carry):
-            action(d)
-            return carry
-
-        lax.fori_loop(1, facets, step, 0)
+            src_ref=send2.at[peer(d)], dst_ref=recv2.at[d], send_sem=send_sem2.at[d],
+            recv_sem=recv_sem2.at[d], device_id={"facet": peer(d)},
+            device_id_type=pl.DeviceIdType.MESH,
+        )
+
+    order = list(range(half, facets)) + list(range(1, half))
 
     position = iota((1, strip), 1)
     taper[...] = sine((position.astype(F32) + 0.5) * (math.pi / strip)) * (1.0 / math.sqrt(strip))
-    frequency = iota((XC, LANES), 0)
+    frequency = iota((LANES, XC), 1)
     first = (2 * me + 1) * (strip // facets)
-    start = turn(frequency * (iota((XC, LANES), 1) + first), strip)
+    start = turn(frequency * (iota((LANES, XC), 0) + first), strip)
     step_cos, step_sin = turn(frequency * LANES, strip)
     for copy in small:
         copy.wait()
     offset = jnp.zeros((slots, strip), jnp.int32)
     slot_row = iota((slots, strip), 0)
     for i in range(slots):
-        offset = jnp.where(slot_row == i, offsets[owner[i]], offset)
+        offset = jnp.where(slot_row == i, offsets[owner[peer(i)]], offset)
     shift_cos, shift_sin = turn(offset * iota((slots, strip), 1), strip)
     shift[0] = shift_cos
     shift[1] = -shift_sin
     sky_copy.wait()
     windowed[...] = (sky[...].astype(F32) * taper[...]).astype(BF16).astype(F32)
-    total[...] = jnp.zeros_like(total)
-
-    def contribute(group, carry):
-        c, s = carry
-        bases, pieces = [], []
-        for member in range(GROUP):
-            block = group * GROUP + member
-            upper = jnp.concatenate([c, s], axis=1)
-            lower = jnp.concatenate([-s, c], axis=1)
-            base = jnp.concatenate([upper, lower], axis=0).astype(BF16)
-            table[block] = base
-            bases.append(base)
-            rows = pl.ds(pl.multiple_of(block * LANES, LANES), LANES)
-            piece = windowed[:, rows]
-            real, imag = shift[0, :, rows], shift[1, :, rows]
-            pieces.append(
-                jnp.concatenate(
-                    [
-                        jnp.concatenate(
-                            [real[i : i + 1] * piece, imag[i : i + 1] * piece], axis=1
-                        ).astype(BF16)
-                        for i in range(slots)
-                    ],
-                    axis=0,
+    def contribute(lowest, make_table):
+        c, s = start
+        total = jnp.zeros((half * columns, 2 * XC), F32)
+        for group in range(blocks // GROUP):
+            pieces = []
+            for block in range(group * GROUP, (group + 1) * GROUP):
+                if make_table:
+                    left_part = jnp.concatenate([c, s], axis=0)
+                    right_part = jnp.concatenate([-s, c], axis=0)
+                    across[pl.ds(block * 2 * LANES, 2 * LANES)] = jnp.concatenate(
+                        [left_part, right_part], axis=1
+                    ).astype(BF16)
+                    c, s = c * step_cos - s * step_sin, s * step_cos + c * step_sin
+                rows = slice(block * LANES, (block + 1) * LANES)
+                piece = windowed[:, rows]
+                real, imag = shift[0, :, rows], shift[1, :, rows]
+                pieces.append(
+                    jnp.concatenate(
+                        [
+                            jnp.concatenate(
+                                [real[i : i + 1] * piece, imag[i : i + 1] * piece], axis=1
+                            ).astype(BF16)
+                            for i in range(lowest, lowest + half)
+                        ],
+                        axis=0,
+                    )
                 )
+            depth = GROUP * 2 * LANES
+            total = total + jnp.dot(
+                jnp.concatenate(pieces, axis=1), across[pl.ds(group * depth, depth)],
+                preferred_element_type=F32,
             )
-            c, s = c * step_cos - s * step_sin, s * step_cos + c * step_sin
-        total[...] += lax.dot_general(
-            jnp.concatenate(pieces, axis=1), jnp.concatenate(bases, axis=1), NT,
-            preferred_element_type=F32,
-        )
-        return c, s
-
-    lax.fori_loop(0, blocks // GROUP, contribute, start)
-    send1[...] = total[...].astype(BF16).reshape(send1.shape)
-
+        send1[lowest : lowest + half] = total.astype(BF16).reshape(half, columns, 2 * XC)
+
+    contribute(half, True)
     pl.semaphore_wait(barrier, facets + 1)
-    each(lambda d: out1(d).start())
-    recv1[me] = send1[me]
+    for d in range(half, facets):
+        send_contribution(d).start()
+    contribute(0, False)
+    for d in range(1, half):
+        send_contribution(d).start()
+    recv1[me] = send1[0]
     early = [
         exchange(0, obs_hbm.at[0, :, pl.ds(columns - 2 * EDGE, 2 * EDGE)], obs_halo.at[0], right),
         exchange(1, obs_hbm.at[0, :, pl.ds(0, 2 * EDGE)], obs_halo.at[1], left),
@@ -217,6 +219,7 @@
     degrid = jnp.zeros((SG, live_slots), F32)
     for t in range(taps):
         degrid = jnp.where(distance == t, rowk[t], degrid)
+    degrid_back = jnp.transpose(degrid).astype(BF16)
     degrid = degrid.astype(BF16)
     grid_cos = jnp.dot(fine_cos, degrid, preferred_element_type=F32)
     grid_sin = jnp.dot(fine_sin, degrid, preferred_element_type=F32)
@@ -225,7 +228,23 @@
     grid[SG:, 0:live_slots] = (-grid_sin).astype(BF16)
     grid[SG:, live_slots:] = grid_cos.astype(BF16)
 
-    each(lambda d: in1(d).wait_recv())
+    grid_cos = jnp.dot(degrid_back, fine_cos, preferred_element_type=F32)
+    grid_sin = jnp.dot(degrid_back, fine_sin, preferred_element_type=F32)
+    back_table[0:live_slots, 0:SG] = grid_cos.astype(BF16)
+    back_table[0:live_slots, SG:] = (-grid_sin).astype(BF16)
+    back_table[live_slots:, 0:SG] = grid_sin.astype(BF16)
+    back_table[live_slots:, SG:] = grid_cos.astype(BF16)
+
+    c, s = jnp.transpose(start[0]), jnp.transpose(start[1])
+    turn_cos, turn_sin = jnp.transpose(step_cos), jnp.transpose(step_sin)
+    for block in range(blocks):
+        upper = jnp.concatenate([c, s], axis=1)
+        lower = jnp.concatenate([-s, c], axis=1)
+        table[block] = jnp.concatenate([upper, lower], axis=0).astype(BF16)
+        c, s = c * turn_cos - s * turn_sin, s * turn_cos + c * turn_sin
+
+    for d in order:
+        take_contribution(d).wait_recv()
     blank = jnp.zeros((columns, SG - XC), F32)
     sums = [jnp.zeros((columns, SG), F32), jnp.zeros((columns, SG), F32)]
     for f in range(facets):
@@ -274,7 +293,7 @@
         parts.append(weight * (seen - model[:, p * live_slots : (p + 1) * live_slots]))
         residual[0, p] = parts[p][EDGE : EDGE + columns]
     rounded = jnp.concatenate(parts, axis=1).astype(BF16)
-    gridded = lax.dot_general(rounded, grid[...], NT, preferred_element_type=F32)
+    gridded = jnp.dot(rounded, back_table[...], preferred_element_type=F32)
     back = jnp.zeros_like(gridded)
     for t in range(taps):
         back = back + colk[t] * pltpu.roll(gridded, (t - margin) % rows, 0)
@@ -288,15 +307,18 @@
             ],
             axis=1,
         ).astype(BF16)
-    each(lambda d: out2(d).start())
-    recv2[me] = send2[me]
+    for d in order:
+        send_pieces(d).start()
+    recv2[0] = send2[me]
     for copy in early + late:
         copy.wait_send()
-    each(lambda d: out1(d).wait_send())
-    each(lambda d: in2(d).wait_recv())
-
+    for d in order:
+        send_contribution(d).wait_send()
+    for d in order:
+        take_pieces(d).wait_recv()
     collected[...] = recv2[...]
-    each(lambda d: out2(d).wait_send())
+    for d in order:
+        send_pieces(d).wait_send()
 
 
 def image_kernel(
@@ -368,10 +390,11 @@
             pltpu.VMEM((2, 2, 2 * EDGE, live_slots), BF16),
             pltpu.VMEM((2, EDGE, live_slots), F32),
             pltpu.VMEM((columns, strip), F32),
-            pltpu.VMEM((slots * columns, 2 * XC), F32),
+            pltpu.VMEM((2 * strip, 2 * XC), BF16),
             traded,
             traded,
             pltpu.VMEM((2 * SG, 2 * live_slots), BF16),
+            pltpu.VMEM((2 * live_slots, 2 * SG), BF16),
             pltpu.VMEM((columns, 2 * SG), F32),
             pltpu.VMEM((2, EDGE, 2 * SG), F32),
             traded,

time: 21.3 us -> 21.5 us (level)
  Pallas kernels: 19.8 us -> 20.1 us
    pallas_call x1, Pallas kernels: 18.4 us -> 18.7 us  [local(): pl.pallas_call(functools.partial(kernel, facets, bands), out_shape=(pltpu...]
where the time goes in v4:
time: 21.5 us; the launch traced here: 21.3 us
  Pallas kernels  20.1 us (93%)
  between operations  1.29 us (6%)
    pallas_call x1, Pallas kernels, local(): pl.pallas_call(functools.partial(kernel, facets, bands), out_shape=(pltpu...  18.7 us
    pallas_call x1, Pallas kernels, local(): pl.pallas_call(image_kernel, out_shape=(jax.ShapeDtypeStruct(observed.sha...  1.39 us

profile of v4, /device:TPU:1, one launch (start us, length us, event | category | flops | bytes accessed | tf_op | source)
XLA Modules:
  0.0 21.3 jit_solution(13577851663972460220)
XLA Ops:
  1.3 18.7 %shard_map.104 = (f32[1,2,32,512]{3,2,1,0:T(8,128)S(1)}, bf16[8,32,256]{2,1,0:T(8,128)(2,1)S(1)}, bf16[16,256,256]{2,1,0:T(8,128)(2,1)S(1)}, f32[2,8,2048]{2,1,0:T(8,128)S(1)}, f32[1,2048]{1,0:T(1,128)S(1)}) custom-call(s32[8]{0:T(128)} %offsets_hbm.1, s32[8]{0:T(128)} %owner_hbm.1, s32[1]{0:T(128)S(6)} %copy.11.count_hbm, f32[7]{0:T(128)} %rowk_hbm.1, ...), custom_call_target="tpu_custom_call" | custom-call | tf_op jit(solution)/shard_map/pallas_call | solution.py:369
  19.9 1.4 %shard_map.105 = (f32[1,2,32,512]{3,2,1,0:T(8,128)}, f32[32,2048]{1,0:T(8,128)}) custom-call(f32[1,2,32,512]{3,2,1,0:T(8,128)S(1)} %get-tuple-element.7.residual, bf16[8,32,256]{2,1,0:T(8,128)(2,1)S(1)} %get-tuple-element.8.collected, bf16[16,256,256]{2,1,0:T(8,128)(2,1)S(1)} %get-tuple-element.9.table, f32[2,8,2048]{2,1,0:T(8,128)S(1)} %get-tuple-element.10.shift, ...), custom_call_target="tpu_custom_call" | custom-call | tf_op jit(solution)/shard_map/pallas_call | solution.py:418

commit v5 on v4

--- a/solution.py
+++ b/solution.py
@@ -13,6 +13,7 @@
 LANES = 128
 EDGE = 8
 GROUP = 4
+STEP = 16
 F32 = jnp.float32
 BF16 = jnp.bfloat16
 
@@ -148,16 +149,20 @@
     frequency = iota((LANES, XC), 1)
     first = (2 * me + 1) * (strip // facets)
     start = turn(frequency * (iota((LANES, XC), 0) + first), strip)
-    step_cos, step_sin = turn(frequency * LANES, strip)
+    step_cos, step_sin = turn(frequency[0:1] * LANES, strip)
     for copy in small:
         copy.wait()
-    offset = jnp.zeros((slots, strip), jnp.int32)
-    slot_row = iota((slots, strip), 0)
+    offset = jnp.zeros((slots, LANES), jnp.int32)
+    slot_row = iota((slots, LANES), 0)
     for i in range(slots):
         offset = jnp.where(slot_row == i, offsets[owner[peer(i)]], offset)
-    shift_cos, shift_sin = turn(offset * iota((slots, strip), 1), strip)
-    shift[0] = shift_cos
-    shift[1] = -shift_sin
+    c, s = turn(offset * iota((slots, LANES), 1), strip)
+    ahead_cos, ahead_sin = turn(offset * LANES, strip)
+    for block in range(blocks):
+        rows = slice(block * LANES, (block + 1) * LANES)
+        shift[0, :, rows] = c
+        shift[1, :, rows] = -s
+        c, s = c * ahead_cos - s * ahead_sin, s * ahead_cos + c * ahead_sin
     sky_copy.wait()
     windowed[...] = (sky[...].astype(F32) * taper[...]).astype(BF16).astype(F32)
     def contribute(lowest, make_table):
@@ -212,14 +217,19 @@
         copy.start()
 
     factor = 1.0 / math.sqrt(facets * XC)
-    fine_cos, fine_sin = turn(iota((SG, SG), 0) * iota((SG, SG), 1), SG)
-    fine_cos = (fine_cos * factor).astype(BF16)
-    fine_sin = (fine_sin * factor).astype(BF16)
+    c, s = turn(iota((STEP, SG), 0) * iota((STEP, SG), 1), SG)
+    c, s = c * factor, s * factor
+    ahead_cos, ahead_sin = turn(iota((1, SG), 1) * STEP, SG)
+    cosines, sines = [], []
+    for _ in range(SG // STEP):
+        cosines.append(c.astype(BF16))
+        sines.append(s.astype(BF16))
+        c, s = c * ahead_cos - s * ahead_sin, s * ahead_cos + c * ahead_sin
+    fine_cos, fine_sin = jnp.concatenate(cosines, axis=0), jnp.concatenate(sines, axis=0)
     distance = iota((SG, live_slots), 0) - cell[...] + margin
     degrid = jnp.zeros((SG, live_slots), F32)
     for t in range(taps):
         degrid = jnp.where(distance == t, rowk[t], degrid)
-    degrid_back = jnp.transpose(degrid).astype(BF16)
     degrid = degrid.astype(BF16)
     grid_cos = jnp.dot(fine_cos, degrid, preferred_element_type=F32)
     grid_sin = jnp.dot(fine_sin, degrid, preferred_element_type=F32)
@@ -227,21 +237,6 @@
     grid[0:SG, live_slots:] = grid_sin.astype(BF16)
     grid[SG:, 0:live_slots] = (-grid_sin).astype(BF16)
     grid[SG:, live_slots:] = grid_cos.astype(BF16)
-
-    grid_cos = jnp.dot(degrid_back, fine_cos, preferred_element_type=F32)
-    grid_sin = jnp.dot(degrid_back, fine_sin, preferred_element_type=F32)
-    back_table[0:live_slots, 0:SG] = grid_cos.astype(BF16)
-    back_table[0:live_slots, SG:] = (-grid_sin).astype(BF16)
-    back_table[live_slots:, 0:SG] = grid_sin.astype(BF16)
-    back_table[live_slots:, SG:] = grid_cos.astype(BF16)
-
-    c, s = jnp.transpose(start[0]), jnp.transpose(start[1])
-    turn_cos, turn_sin = jnp.transpose(step_cos), jnp.transpose(step_sin)
-    for block in range(blocks):
-        upper = jnp.concatenate([c, s], axis=1)
-        lower = jnp.concatenate([-s, c], axis=1)
-        table[block] = jnp.concatenate([upper, lower], axis=0).astype(BF16)
-        c, s = c * turn_cos - s * turn_sin, s * turn_cos + c * turn_sin
 
     for d in order:
         take_contribution(d).wait_recv()
@@ -260,6 +255,15 @@
     ]
     for copy in late:
         copy.start()
+
+    degrid_back = jnp.transpose(degrid.astype(F32)).astype(BF16)
+    grid_cos = jnp.dot(degrid_back, fine_cos, preferred_element_type=F32)
+    grid_sin = jnp.dot(degrid_back, fine_sin, preferred_element_type=F32)
+    back_table[0:live_slots, 0:SG] = grid_cos.astype(BF16)
+    back_table[0:live_slots, SG:] = (-grid_sin).astype(BF16)
+    back_table[live_slots:, 0:SG] = grid_sin.astype(BF16)
+    back_table[live_slots:, SG:] = grid_cos.astype(BF16)
+
 
     obs_copy.wait()
     wt_copy.wait()
@@ -310,6 +314,16 @@
     for d in order:
         send_pieces(d).start()
     recv2[0] = send2[me]
+
+    c, s = jnp.transpose(start[0]), jnp.transpose(start[1])
+    turn_cos = jnp.transpose(jnp.broadcast_to(step_cos, (LANES, XC)))
+    turn_sin = jnp.transpose(jnp.broadcast_to(step_sin, (LANES, XC)))
+    for block in range(blocks):
+        upper = jnp.concatenate([c, s], axis=1)
+        lower = jnp.concatenate([-s, c], axis=1)
+        table[block] = jnp.concatenate([upper, lower], axis=0).astype(BF16)
+        c, s = c * turn_cos - s * turn_sin, s * turn_cos + c * turn_sin
+
     for copy in early + late:
         copy.wait_send()
     for d in order:

time: 21.5 us -> 21.7 us (level)
  no operation moved by 1% of the time
where the time goes in v5:
time: 21.7 us; the launch traced here: 21.5 us
  Pallas kernels  20.2 us (93%)
  between operations  1.29 us (6%)
    pallas_call x1, Pallas kernels, local(): pl.pallas_call(functools.partial(kernel, facets, bands), out_shape=(pltpu...  18.8 us
    pallas_call x1, Pallas kernels, local(): pl.pallas_call(image_kernel, out_shape=(jax.ShapeDtypeStruct(observed.sha...  1.39 us

profile of v5, /device:TPU:1, one launch (start us, length us, event | category | flops | bytes accessed | tf_op | source)
XLA Modules:
  0.0 21.5 jit_solution(14942654218482686954)
XLA Ops:
  1.3 18.8 %shard_map.104 = (f32[1,2,32,512]{3,2,1,0:T(8,128)S(1)}, bf16[8,32,256]{2,1,0:T(8,128)(2,1)S(1)}, bf16[16,256,256]{2,1,0:T(8,128)(2,1)S(1)}, f32[2,8,2048]{2,1,0:T(8,128)S(1)}, f32[1,2048]{1,0:T(1,128)S(1)}) custom-call(s32[8]{0:T(128)} %offsets_hbm.1, s32[8]{0:T(128)} %owner_hbm.1, s32[1]{0:T(128)S(6)} %copy.11.count_hbm, f32[7]{0:T(128)} %rowk_hbm.1, ...), custom_call_target="tpu_custom_call" | custom-call | tf_op jit(solution)/shard_map/pallas_call | solution.py:383
  20.1 1.4 %shard_map.105 = (f32[1,2,32,512]{3,2,1,0:T(8,128)}, f32[32,2048]{1,0:T(8,128)}) custom-call(f32[1,2,32,512]{3,2,1,0:T(8,128)S(1)} %get-tuple-element.7.residual, bf16[8,32,256]{2,1,0:T(8,128)(2,1)S(1)} %get-tuple-element.8.collected, bf16[16,256,256]{2,1,0:T(8,128)(2,1)S(1)} %get-tuple-element.9.table, f32[2,8,2048]{2,1,0:T(8,128)S(1)} %get-tuple-element.10.shift, ...), custom_call_target="tpu_custom_call" | custom-call | tf_op jit(solution)/shard_map/pallas_call | solution.py:432

commit v6 on v5

--- a/solution.py
+++ b/solution.py
@@ -47,10 +47,32 @@
     return lax.broadcasted_iota(jnp.int32, shape, dim)
 
 
+def image_sum(pieces, lowest, table, shift, target, finish, store):
+    slots, columns = pieces.shape[:2]
+    pieces = pieces.reshape(slots * columns, pieces.shape[2])
+    for block in range(table.shape[0]):
+        rows = slice(block * LANES, (block + 1) * LANES)
+        back_rows = jnp.dot(pieces, table[block], preferred_element_type=F32)
+        real = shift[0, lowest : lowest + slots, rows]
+        imag = shift[1, lowest : lowest + slots, rows]
+        strip_sum = jnp.zeros((columns, LANES), F32)
+        if finish is not None:
+            strip_sum = finish[0][:, rows]
+        for i in range(slots):
+            own = back_rows[i * columns : (i + 1) * columns]
+            strip_sum = strip_sum + real[i : i + 1] * own[:, :LANES]
+            strip_sum = strip_sum + imag[i : i + 1] * own[:, LANES:]
+        if finish is not None:
+            strip_sum = strip_sum * finish[1][:, rows]
+        target[:, rows] = strip_sum
+        if store is not None:
+            store(block)
+
+
 def kernel(
     facets, bands, offsets_hbm, owner_hbm, count_hbm, rowk_hbm, colk_hbm, cell_hbm,
     sky_hbm, obs_hbm, wt_hbm,
-    residual, collected, table, shift, taper,
+    residual, collected, partial, table, shift, taper,
     offsets, owner, count, rowk, colk, cell, sky, obs, wt, obs_halo, wt_halo, windowed, across,
     send1, recv1, grid, back_table, z, z_halo, send2, recv2,
     local_sem, send_sem1, recv_sem1, send_sem2, recv_sem2, halo_send, halo_recv,
@@ -328,37 +350,35 @@
         copy.wait_send()
     for d in order:
         send_contribution(d).wait_send()
-    for d in order:
+    for d in range(1, half):
         take_pieces(d).wait_recv()
-    collected[...] = recv2[...]
+    image_sum(recv2[0:half], 0, table, shift, partial, None, None)
+    for d in range(half, facets):
+        take_pieces(d).wait_recv()
+    collected[...] = recv2[half:facets]
     for d in order:
         send_pieces(d).wait_send()
 
 
 def image_kernel(
-    residual, collected, table, shift, taper, residual_hbm, dirty_hbm, dirty, sem
+    residual, collected, partial, table, shift, taper, residual_hbm, dirty_hbm, dirty, sem
 ):
-    slots, columns = collected.shape[:2]
-    strip = taper.shape[1]
-    groups = strip // LANES // GROUP
+    groups = taper.shape[1] // LANES // GROUP
     residual_copy = pltpu.make_async_copy(residual, residual_hbm, sem.at[groups])
     residual_copy.start()
-    pieces = collected[...].reshape(slots * columns, 2 * XC)
     copies = []
-    for group in range(groups):
-        for block in range(group * GROUP, (group + 1) * GROUP):
-            rows = slice(block * LANES, (block + 1) * LANES)
-            back_rows = jnp.dot(pieces, table[block], preferred_element_type=F32)
-            real, imag = shift[0, :, rows], shift[1, :, rows]
-            strip_sum = jnp.zeros((columns, LANES), F32)
-            for i in range(slots):
-                own = back_rows[i * columns : (i + 1) * columns]
-                strip_sum = strip_sum + real[i : i + 1] * own[:, :LANES]
-                strip_sum = strip_sum + imag[i : i + 1] * own[:, LANES:]
-            dirty[:, rows] = strip_sum * taper[:, rows]
-        rows = pl.ds(group * GROUP * LANES, GROUP * LANES)
-        copies.append(pltpu.make_async_copy(dirty.at[:, rows], dirty_hbm.at[:, rows], sem.at[group]))
-        copies[-1].start()
+
+    def store(block):
+        if (block + 1) % GROUP == 0:
+            group = block // GROUP
+            rows = pl.ds(group * GROUP * LANES, GROUP * LANES)
+            copies.append(
+                pltpu.make_async_copy(dirty.at[:, rows], dirty_hbm.at[:, rows], sem.at[group])
+            )
+            copies[-1].start()
+
+    lowest = shift.shape[1] - collected.shape[0]
+    image_sum(collected[...], lowest, table, shift, dirty, (partial, taper), store)
     for copy in copies:
         copy.wait()
     residual_copy.wait()
@@ -384,13 +404,14 @@
         functools.partial(kernel, facets, bands),
         out_shape=(
             pltpu.VMEM(observed.shape, F32),
-            pltpu.VMEM((facets, columns, 2 * XC), BF16),
+            pltpu.VMEM((facets - facets // 2, columns, 2 * XC), BF16),
+            pltpu.VMEM((columns, strip), F32),
             pltpu.VMEM((strip // LANES, 2 * XC, 2 * LANES), BF16),
             pltpu.VMEM((2, slots, strip), F32),
             pltpu.VMEM((1, strip), F32),
         ),
         in_specs=[hbm] * 9,
-        out_specs=(vmem,) * 5,
+        out_specs=(vmem,) * 6,
         scratch_shapes=[
             pltpu.SMEM(subgrid_offsets.shape, jnp.int32),
             pltpu.SMEM(owner_order.shape, jnp.int32),
@@ -435,7 +456,7 @@
             jax.ShapeDtypeStruct(observed.shape, F32),
             jax.ShapeDtypeStruct(sky_image.shape, F32),
         ),
-        in_specs=[vmem] * 5,
+        in_specs=[vmem] * 6,
         out_specs=(hbm, hbm),
         scratch_shapes=[
             pltpu.VMEM((columns, strip), F32),

time: 21.7 us -> 21.4 us (0.986)
  Pallas kernels: 20.2 us -> 19.9 us
    pallas_call x1, Pallas kernels: 1.39 us -> 1.13 us  [local(): pl.pallas_call(image_kernel, out_shape=(jax.ShapeDtypeStruct(observed.sha...]
where the time goes in v6:
time: 21.4 us; the launch traced here: 21.2 us
  Pallas kernels  19.9 us (93%)
  between operations  1.29 us (6%)
    pallas_call x1, Pallas kernels, local(): pl.pallas_call(functools.partial(kernel, facets, bands), out_shape=(pltpu...  18.8 us
    pallas_call x1, Pallas kernels, local(): pl.pallas_call(image_kernel, out_shape=(jax.ShapeDtypeStruct(observed.sha...  1.13 us

profile of v6, /device:TPU:1, one launch (start us, length us, event | category | flops | bytes accessed | tf_op | source)
XLA Modules:
  0.0 21.2 jit_solution(8839911819224090228)
XLA Ops:
  1.3 18.8 %shard_map.104 = (f32[1,2,32,512]{3,2,1,0:T(8,128)S(1)}, bf16[4,32,256]{2,1,0:T(8,128)(2,1)S(1)}, f32[32,2048]{1,0:T(8,128)S(1)}, bf16[16,256,256]{2,1,0:T(8,128...) custom-call(s32[8]{0:T(128)} %offsets_hbm.1, s32[8]{0:T(128)} %owner_hbm.1, s32[1]{0:T(128)S(6)} %copy.11.count_hbm, ...), custom_call_target="tpu_custom_call" | custom-call | tf_op jit(solution)/shard_map/pallas_call | solution.py:403
  20.1 1.1 %shard_map.105 = (f32[1,2,32,512]{3,2,1,0:T(8,128)}, f32[32,2048]{1,0:T(8,128)}) custom-call(f32[1,2,32,512]{3,2,1,0:T(8,128)S(1)} %get-tuple-element.8.residual, bf16[4,32,256]{2,1,0:T(8,128)(2,1)S(1)} %get-tuple-element.9.collected, f32[32,2048]{1,0:T(8,128)S(1)} %get-tuple-element.10.partial, bf16[16,256,256]{2,1,0:T(8,128)(2,1)S(1)} %get-tuple-element.11.table, ...), custom_call_target="tpu_custom_call" | custom-call | tf_op jit(solution)/shard_map/pallas_call | solution.py:453
